TPU v7x, 128 devices: a whole 4x4x4 slice. The times are simulated.
128 devices in a mesh: space: 32 (over y, z_lo, x), group: 4 (over z_hi, core).
Axes of the slice: x: 4, y: 4, z: 4 (z_hi: 2, z_lo: 2; z = z_hi * 2 + z_lo), core: 2. Of those that a mesh axis runs over, the one named last changes fastest.
Arguments:
- source: float32 [512, 256, 256], P('space', 'group'), may hold values from -4.5 to 6.5
- phases: int32 [512, 256, 256], P('space', 'group'), may hold values from 0 to 7
Outputs:
- pressure: float32 [512, 256, 256], P('space', 'group')
- residual: float32 [512, 256, 256], P('space', 'group')
All inputs are finite; a program needn't handle non-finite values.
Results may differ from a plain program's by a relative error of at most 0.0003.
Values sent between devices are 32-bit elements; how exact they have to be, the bound alone decides.
A program may use at most 192 MiB of HBM per device.

v0:
```python
import math

import jax
import jax.numpy as jnp
from jax import lax
from jax.sharding import PartitionSpec as P

PRE = 2
POST = 2
CHEB = 6
PHASES = 8


REACTION = 0.01
RELAX = 0.8
LOWER = 0.05
UPPER = 2.0


def with_halo(cells, sides, width):
    for axis, dim in sides:
        count = lax.axis_size(axis)
        ends = count - 1
        head = lax.slice_in_dim(cells, 0, width, axis=dim)
        tail = lax.slice_in_dim(cells, cells.shape[dim] - width, cells.shape[dim], axis=dim)
        cells = jnp.concatenate(
            [
                lax.ppermute(tail, axis, [(i, (i + 1) % count) for i in range(ends)]),
                cells,
                lax.ppermute(head, axis, [((i + 1) % count, i) for i in range(ends)]),
            ],
            axis=dim,
        )
    return cells


def conductivity(phases):
    return jnp.exp(phases.astype(jnp.float32) * (-6.0 * math.log(10.0) / (PHASES - 1)))


def harmonic(left, right):
    total = left + right
    return 2.0 * left * right / jnp.where(total > 0.0, total, 1.0)


def face_weights(kpadded):
    center = kpadded[1:-1, 1:-1, 1:-1]
    return (
        harmonic(center, kpadded[2:, 1:-1, 1:-1]),
        harmonic(center, kpadded[:-2, 1:-1, 1:-1]),
        harmonic(center, kpadded[1:-1, 2:, 1:-1]),
        harmonic(center, kpadded[1:-1, :-2, 1:-1]),
        harmonic(center, kpadded[1:-1, 1:-1, 2:]),
        harmonic(center, kpadded[1:-1, 1:-1, :-2]),
    )


def stencil(center, padded, weights):
    field = padded[1:-1, 1:-1, 1:-1]
    beside_all = weights[0] * padded[2:, 1:-1, 1:-1] + weights[1] * padded[:-2, 1:-1, 1:-1]
    beside_all = (
        beside_all + weights[2] * padded[1:-1, 2:, 1:-1] + weights[3] * padded[1:-1, :-2, 1:-1]
    )
    beside_all = (
        beside_all + weights[4] * padded[1:-1, 1:-1, 2:] + weights[5] * padded[1:-1, 1:-1, :-2]
    )
    return center * field - beside_all


def collapse_x(array):
    extent = array.shape
    return array.reshape(extent[0], extent[1] // 2, 2, extent[2] // 2, 2).sum(axis=(2, 4))


def collapse_y(array):
    extent = array.shape
    return array.reshape(extent[0] // 2, 2, extent[1], extent[2] // 2, 2).sum(axis=(1, 4))


def collapse_z(array):
    extent = array.shape
    return array.reshape(extent[0] // 2, 2, extent[1] // 2, 2, extent[2]).sum(axis=(1, 3))


def collapse_all(array):
    extent = array.shape
    return array.reshape(extent[0] // 2, 2, extent[1] // 2, 2, extent[2] // 2, 2).sum(
        axis=(1, 3, 5)
    )


def coarse_operator(kappa, weights):
    east = collapse_x(weights[0][1::2])
    west = collapse_x(weights[1][0::2])
    north = collapse_y(weights[2][:, 1::2])
    south = collapse_y(weights[3][:, 0::2])
    upper = collapse_z(weights[4][:, :, 1::2])
    lower = collapse_z(weights[5][:, :, 0::2])
    center = collapse_all(REACTION * kappa) + east + west + north + south + upper + lower
    return (east, west, north, south, upper, lower, center)


def expand_blocks(coarse):
    extent = coarse.shape
    spread = jnp.broadcast_to(
        coarse[:, None, :, None, :, None], (extent[0], 2, extent[1], 2, extent[2], 2)
    )
    return spread.reshape(2 * extent[0], 2 * extent[1], 2 * extent[2])


def chebyshev(forcing, coefs, padder):
    weights = coefs[:6]
    center = coefs[6]
    theta = (UPPER + LOWER) / 2.0
    delta = (UPPER - LOWER) / 2.0
    ratio = delta / theta
    correction = jnp.zeros_like(forcing)
    remainder = forcing
    heading = remainder / center * (1.0 / theta)
    for turn in range(CHEB):
        correction = correction + heading
        if turn + 1 < CHEB:
            remainder = remainder - stencil(center, padder(heading), weights)
            following = 1.0 / (2.0 * theta / delta - ratio)
            heading = following * ratio * heading + 2.0 * following / delta * (remainder / center)
            ratio = following
    return correction


def pad_space(field):
    rimmed = with_halo(field, (("space", 0),), 1)
    return jnp.pad(rimmed, ((0, 0), (1, 1), (1, 1)))


def per_device(source, phases):
    total = lax.psum(jnp.sum(source), ("space", "group"))
    cells = source.size * lax.axis_size("space") * lax.axis_size("group")
    average = total / cells
    kappa = conductivity(phases)
    kappa_halo = with_halo(kappa, (("space", 0), ("group", 1)), 1)
    weights = face_weights(jnp.pad(kappa_halo, ((0, 0), (0, 0), (1, 1))))
    diagonal = (
        REACTION * kappa
        + weights[0]
        + weights[1]
        + weights[2]
        + weights[3]
        + weights[4]
        + weights[5]
    )
    forcing = kappa * (source - average)
    coefs = coarse_operator(kappa, weights)

    def residual_of(current):
        rimmed = with_halo(current, (("space", 0), ("group", 1)), 1)
        padded = jnp.pad(rimmed, ((0, 0), (0, 0), (1, 1)))
        return forcing - stencil(diagonal, padded, weights)

    def relax(current, remainder):
        return current + RELAX * (remainder / diagonal)

    pressure = jnp.zeros(source.shape, jnp.float32)
    residual = forcing
    for sweep in range(PRE):
        pressure = relax(pressure, residual)
        residual = residual_of(pressure)
    coarse_forcing = collapse_all(residual)
    moved = (
        lax.all_gather(coarse_forcing, "group", axis=1, tiled=True),
        lax.all_gather(coefs[0], "group", axis=1, tiled=True),
        lax.all_gather(coefs[1], "group", axis=1, tiled=True),
        lax.all_gather(coefs[2], "group", axis=1, tiled=True),
        lax.all_gather(coefs[3], "group", axis=1, tiled=True),
        lax.all_gather(coefs[4], "group", axis=1, tiled=True),
        lax.all_gather(coefs[5], "group", axis=1, tiled=True),
        lax.all_gather(coefs[6], "group", axis=1, tiled=True),
    )
    whole_forcing = moved[0]
    whole_coefs = moved[1:]
    whole_correction = chebyshev(whole_forcing, whole_coefs, pad_space)
    width = coarse_forcing.shape[1]
    correction = lax.dynamic_slice_in_dim(
        whole_correction, lax.axis_index("group") * width, width, 1
    )
    pressure = pressure + expand_blocks(correction)
    residual = residual_of(pressure)
    for sweep in range(POST):
        pressure = relax(pressure, residual)
        residual = residual_of(pressure)
    return (pressure, residual)


def solution(mesh):
    in_specs = (P("space", "group", None), P("space", "group", None))
    out_specs = (P("space", "group", None), P("space", "group", None))
    return jax.shard_map(
        per_device, mesh=mesh, in_specs=in_specs, out_specs=out_specs, check_vma=False
    )
```

profile of v0, /device:TPU:9, one launch (start us, length us, event | category | flops | bytes accessed | tf_op | source)
XLA Modules:
  0.0 745.7 jit_solution(12321833456175638661)
XLA Ops:
  2.1 3.1 collective-permute-start.1
  5.3 5.2 collective-permute-start
  11.8 7.2 collective-permute-start.3
  22.0 66.2 %psum.7 = f32[]{:T(128)} all-reduce(f32[]{:T(128)} %reduce_sum.81), channel_id=1, replica_groups=mesh['space'=32,'group'=4] {'space','group'}, use_global_device_ids=true, to_apply=%region_1.0 | all-reduce | flops 1 | bytes 8 | tf_op jit(solution)/shard_map/psum | solution.py:136
  92.7 5.0 divide_multiply_fusion
  97.6 3.3 slice.459
  100.9 3.0 copy.81
  103.9 4.2 reduce_sum.87
  111.8 19.0 %slice.461 = f32[16,64,128]{2,1,0:T(8,128)} slice(f32[16,64,256]{2,1,0:T(8,128)} %get-tuple-element.35), slice={[0:16:1], [0:64:1], [0:256:2]} | slice | bytes 1048576 | tf_op jit(solution)/shard_map/slice | solution.py:98
  132.4 9.6 %all_gather.31 = f32[8,128,128]{2,0,1:T(8,128)} all-gather(f32[8,32,128]{2,0,1:T(8,128)S(1)} %copy.95), channel_id=1, replica_groups=mesh['space'=32,'group'=4] {'group'}, dimensions={1}, use_global_device_ids=true | all-gather | bytes 655360 | tf_op jit(solution)/shard_map/all_gather | solution.py:175
  142.0 19.0 %slice.460 = f32[16,64,128]{2,1,0:T(8,128)} slice(f32[16,64,256]{2,1,0:T(8,128)} %get-tuple-element.13), slice={[0:16:1], [0:64:1], [1:256:2]} | slice | bytes 1048576 | tf_op jit(solution)/shard_map/slice | solution.py:97
  166.0 6.4 collective-permute-start.4
  172.4 9.2 %all_gather.30 = f32[8,128,128]{2,0,1:T(8,128)} all-gather(f32[8,32,128]{2,0,1:T(8,128)S(1)} %copy.94), channel_id=1, replica_groups=mesh['space'=32,'group'=4] {'group'}, dimensions={1}, use_global_device_ids=true | all-gather | bytes 655360 | tf_op jit(solution)/shard_map/all_gather | solution.py:174
  184.3 3.3 slice.458
  187.6 3.0 copy.79
  190.6 4.2 reduce_sum.86
  196.6 5.9 copy.77
  202.5 10.9 %reduce_sum.85 = f32[8,32,128]{0,2,1:T(8,128)} reduce(f32[8,32,2,128,2]{0,4,3,2,1:T(2,128)} %bitcast.28, f32[]{:T(128)} %constant.23.clone.1), dimensions={2,4}, to_apply=%region_5.6 | reduce | flops 98304 | bytes 655364 | tf_op jit(solution)/shard_map/reduce_sum | solution.py:72
  213.4 2.8 copy.78
  216.2 5.9 copy.75
  222.1 10.9 %reduce_sum.84 = f32[8,32,128]{0,2,1:T(8,128)} reduce(f32[8,32,2,128,2]{0,4,3,2,1:T(2,128)} %bitcast.29, f32[]{:T(128)} %constant.23.clone.1), dimensions={2,4}, to_apply=%region_4.5 | reduce | flops 98304 | bytes 655364 | tf_op jit(solution)/shard_map/reduce_sum | solution.py:72
  233.0 2.8 copy.76
  235.8 69.1 %reshape.33 = f32[8,2,32,2,128,2]{5,4,3,2,1,0:T(8,128)} reshape(f32[16,64,256]{2,1,0:T(8,128)} %get-tuple-element.34) | data formatting | bytes 2097152 | tf_op jit(solution)/shard_map/reshape | solution.py:87
  305.0 21.4 %reduce_sum.83 = f32[8,32,128]{2,1,0:T(8,128)} reduce(f32[8,2,32,2,128,2]{5,4,3,2,1,0:T(8,128)} %reshape.33, f32[]{:T(128)} %constant.23.clone.1), dimensions={1,3,5}, to_apply=%region_3.4 | reduce | flops 229376 | bytes 1179652 | tf_op jit(solution)/shard_map/reduce_sum | solution.py:87
  328.3 9.4 %all_gather.29 = f32[8,128,128]{2,0,1:T(8,128)} all-gather(f32[8,32,128]{2,0,1:T(8,128)} %copy.93), channel_id=1, replica_groups=mesh['space'=32,'group'=4] {'group'}, dimensions={1}, use_global_device_ids=true | all-gather | bytes 655360 | tf_op jit(solution)/shard_map/all_gather | solution.py:173
  340.0 3.5 collective-permute-start.7
  345.4 9.6 %all_gather.28 = f32[8,128,128]{2,0,1:T(8,128)} all-gather(f32[8,32,128]{2,0,1:T(8,128)S(1)} %copy.90), channel_id=1, replica_groups=mesh['space'=32,'group'=4] {'group'}, dimensions={1}, use_global_device_ids=true | all-gather | bytes 655360 | tf_op jit(solution)/shard_map/all_gather | solution.py:172
  359.4 6.8 fusion.65
  368.2 6.4 collective-permute-start.8
  374.6 9.4 %all_gather.27 = f32[8,128,128]{2,0,1:T(8,128)} all-gather(f32[8,32,128]{2,0,1:T(8,128)S(1)} %copy.87), channel_id=1, replica_groups=mesh['space'=32,'group'=4] {'group'}, dimensions={1}, use_global_device_ids=true | all-gather | bytes 655360 | tf_op jit(solution)/shard_map/all_gather | solution.py:171
  384.1 4.0 collective-permute-start.11
  390.1 9.6 %all_gather.25 = f32[8,128,128]{2,0,1:T(8,128)} all-gather(f32[8,32,128]{2,0,1:T(8,128)S(1)} %copy.83), channel_id=1, replica_groups=mesh['space'=32,'group'=4] {'group'}, dimensions={1}, use_global_device_ids=true | all-gather | bytes 655360 | tf_op jit(solution)/shard_map/all_gather | solution.py:176
  404.0 7.6 %fusion.51 = f32[16,64,256]{2,1,0:T(8,128)} fusion(f32[18,66,258]{2,1,0:T(8,128)S(1)} %select_maximum_fusion.22, f32[16,64,256]{2,1,0:T(8,128)} %get-tuple-element.12, f32[18,1,256]{2,1,0:T(1,128)S(1)} %collective-permute-done.11, f32[1,64,256]{2,1,0:T(8,128)S(1)} %collective-permute-done.8, f32[16,64,256]{2,1,0:T(8,128)} %copy-done.16, ...), kind=kLoop, calls=%fused_computation.128 | loop fusion | flops 11534336 | bytes 12750852 | tf_op jit(solution)/shard_map/sub | solution.py:157
  411.6 69.1 %reshape.32 = f32[8,2,32,2,128,2]{5,4,3,2,1,0:T(8,128)} reshape(f32[16,64,256]{2,1,0:T(8,128)} %fusion.51) | data formatting | bytes 2097152 | tf_op jit(solution)/shard_map/reshape | solution.py:87
  480.8 20.8 %reduce_sum.82 = f32[8,32,128]{2,1,0:T(8,128)S(1)} reduce(f32[8,2,32,2,128,2]{5,4,3,2,1,0:T(8,128)} %reshape.32, f32[]{:T(128)} %constant.23.clone.1), dimensions={1,3,5}, to_apply=%region_2.3 | reduce | flops 229376 | bytes 1179652 | tf_op jit(solution)/shard_map/reduce_sum | solution.py:87
  501.6 8.8 %all_gather.24 = f32[8,128,128]{2,0,1:T(8,128)S(1)} all-gather(f32[8,32,128]{2,0,1:T(8,128)S(1)} %copy.74), channel_id=1, replica_groups=mesh['space'=32,'group'=4] {'group'}, dimensions={1}, use_global_device_ids=true | all-gather | bytes 655360 | tf_op jit(solution)/shard_map/all_gather | solution.py:169
  514.0 3.4 collective-permute-start.13
  517.3 9.6 %all_gather.26 = f32[8,128,128]{2,0,1:T(8,128)S(1)} all-gather(f32[8,32,128]{2,0,1:T(8,128)S(1)} %copy.84), channel_id=1, replica_groups=mesh['space'=32,'group'=4] {'group'}, dimensions={1}, use_global_device_ids=true | all-gather | bytes 655360 | tf_op jit(solution)/shard_map/all_gather | solution.py:170
  529.0 4.1 collective-permute-start.14
  535.1 6.1 collective-permute-done.15
  545.2 3.6 collective-permute-start.17
  548.8 4.4 collective-permute-done.17
  553.9 2.5 select_maximum_fusion.4
  556.4 6.1 multiply_add_fusion.1
  565.9 3.4 collective-permute-start.19
  569.2 4.6 collective-permute-done.19
  573.9 2.2 select_maximum_fusion.2
  580.7 3.4 collective-permute-start.21
  584.2 4.6 collective-permute-done.21
  588.8 2.2 select_maximum_fusion
  594.3 21.5 %broadcast_in_dim.16 = f32[8,2,32,2,128,2]{5,4,3,2,1,0:T(8,128)} broadcast(f32[8,32,128]{2,1,0:T(8,128)S(1)} %copy.120), dimensions={0,2,4} | broadcast | bytes 1179648 | tf_op jit(solution)/shard_map/broadcast_in_dim | solution.py:105
  615.8 47.4 %reshape.40 = f32[16,64,256]{2,1,0:T(8,128)} reshape(f32[8,2,32,2,128,2]{5,4,3,2,1,0:T(8,128)} %broadcast_in_dim.16) | data formatting | bytes 2097152 | tf_op jit(solution)/shard_map/reshape | solution.py:108
  666.9 6.6 collective-permute-start.22
  674.9 10.5 %collective-permute-start.25 = (f32[18,1,256]{2,1,0:T(1,128)S(1)}, f32[18,1,256]{2,1,0:T(1,128)S(1)}, u32[]{:S(2)}, u32[]{:S(2)}) collective-permute-start(f32[18,1,256]{2,1,0:T(1,128)S(1)} %get-tuple-element.18), channel_id=1, source_target_pairs={{0,1},{1,2},{2,3},{4,5},{5,6},{6,7},{8,9},{9,10},{10,11},{12,13},{... | collective-permute-start | bytes 55304 | tf_op jit(solution)/shard_map/ppermute | solution.py:28
  687.4 4.6 collective-permute-done.24
  692.8 3.5 fusion.40
  698.3 6.4 collective-permute-start.26
  706.0 3.6 collective-permute-start.29
  711.6 4.6 collective-permute-done.28
  717.1 3.5 fusion.26
  722.6 6.4 collective-permute-start.30
  730.3 3.4 collective-permute-start.33
  735.6 4.6 collective-permute-done.32
  741.1 4.2 fusion.12
  (183 shorter events, 86.0 us)
Async XLA Ops:
  0.6 20.4 %copy-start.1 = (f32[16,64,256]{2,1,0:T(8,128)S(1)}, f32[16,64,256]{2,1,0:T(8,128)}, u32[]{:S(2)}) copy-start(f32[16,64,256]{2,1,0:T(8,128)} %param.2) | copy-start | bytes 3145732
  2.1 16.9 %copy-start.29 = (f32[16,64,256]{2,1,0:T(8,128)}, f32[16,64,256]{2,1,0:T(8,128)S(1)}, u32[]{:S(2)}) copy-start(f32[16,64,256]{2,1,0:T(8,128)S(1)} %multiply_exponential_fusion) | copy-start | bytes 3145732
  2.1 8.3 %collective-permute-start.1 = (f32[1,64,256]{2,1,0:T(8,128)S(1)}, f32[1,64,256]{2,1,0:T(8,128)S(1)}, u32[]{:S(2)}, u32[]{:S(2)}) collective-permute-start(f32[1,64,256]{2,1,0:T(8,128)S(1)} %get-tuple-element.38), channel_id=1, source_target_pairs={{0,4},{4,8},{8,12},{12,16},{16,20},{20,24},{24,28},{28,32},{32,36}... | collective-permute-start | bytes 196616 | tf_op jit(solution)/shard_map/ppermute | solution.py:28
  5.3 6.5 collective-permute-start
  11.8 77.0 %collective-permute-start.3 = (f32[18,1,256]{2,1,0:T(1,128)S(1)}, f32[18,1,256]{2,1,0:T(1,128)S(1)}, u32[]{:S(2)}, u32[]{:S(2)}) collective-permute-start(f32[18,1,256]{2,1,0:T(1,128)S(1)} %get-tuple-element.24), channel_id=1, source_target_pairs={{0,1},{1,2},{2,3},{4,5},{5,6},{6,7},{8,9},{9,10},{10,11},{12,13},{... | collective-permute-start | bytes 55304 | tf_op jit(solution)/shard_map/ppermute | solution.py:28
  19.0 71.8 %copy-start = (s32[16,64,256]{2,1,0:T(8,128)S(1)}, s32[16,64,256]{2,1,0:T(8,128)}, u32[]{:S(2)}) copy-start(s32[16,64,256]{2,1,0:T(8,128)} %param.3) | copy-start | bytes 3145732
  19.0 69.8 %collective-permute-start.2 = (f32[18,1,256]{2,1,0:T(1,128)S(1)}, f32[18,1,256]{2,1,0:T(1,128)S(1)}, u32[]{:S(2)}, u32[]{:S(2)}) collective-permute-start(f32[18,1,256]{2,1,0:T(1,128)S(1)} %get-tuple-element.25), channel_id=1, source_target_pairs={{1,0},{2,1},{3,2},{5,4},{6,5},{7,6},{9,8},{10,9},{11,10},{13,12},{... | collective-permute-start | bytes 55304 | tf_op jit(solution)/shard_map/ppermute | solution.py:30
  162.4 21.1 %copy-start.9 = (f32[16,64,256]{2,1,0:T(8,128)S(1)}, f32[16,64,256]{2,1,0:T(8,128)}, u32[]{:S(2)}) copy-start(f32[16,64,256]{2,1,0:T(8,128)} %get-tuple-element.10) | copy-start | bytes 3145732
  164.1 174.9 %collective-permute-start.5 = (f32[1,64,256]{2,1,0:T(8,128)}, f32[1,64,256]{2,1,0:T(8,128)S(1)}, u32[]{:S(2)}, u32[]{:S(2)}) collective-permute-start(f32[1,64,256]{2,1,0:T(8,128)} %get-tuple-element.36), channel_id=1, source_target_pairs={{0,4},{4,8},{8,12},{12,16},{16,20},{20,24},{24,28},{28,32},{32,36}... | collective-permute-start | bytes 196616 | tf_op jit(solution)/shard_map/ppermute | solution.py:28
  166.0 173.0 %collective-permute-start.4 = (f32[1,64,256]{2,1,0:T(8,128)S(1)}, f32[1,64,256]{2,1,0:T(8,128)S(1)}, u32[]{:S(2)}, u32[]{:S(2)}) collective-permute-start(f32[1,64,256]{2,1,0:T(8,128)S(1)} %get-tuple-element.37), channel_id=1, source_target_pairs={{4,0},{8,4},{12,8},{16,12},{20,16},{24,20},{28,24},{32,28},{36,32}... | collective-permute-start | bytes 196616 | tf_op jit(solution)/shard_map/ppermute | solution.py:30
  340.0 17.2 %collective-permute-start.7 = (f32[18,1,256]{2,1,0:T(1,128)S(1)}, f32[18,1,256]{2,1,0:T(1,128)S(1)}, u32[]{:S(2)}, u32[]{:S(2)}) collective-permute-start(f32[18,1,256]{2,1,0:T(1,128)S(1)} %get-tuple-element.22), channel_id=1, source_target_pairs={{0,1},{1,2},{2,3},{4,5},{5,6},{6,7},{8,9},{9,10},{10,11},{12,13},{... | collective-permute-start | bytes 55304 | tf_op jit(solution)/shard_map/ppermute | solution.py:28
  343.5 13.7 %collective-permute-start.6 = (f32[18,1,256]{2,1,0:T(1,128)S(1)}, f32[18,1,256]{2,1,0:T(1,128)S(1)}, u32[]{:S(2)}, u32[]{:S(2)}) collective-permute-start(f32[18,1,256]{2,1,0:T(1,128)S(1)} %get-tuple-element.23), channel_id=1, source_target_pairs={{1,0},{2,1},{3,2},{5,4},{6,5},{7,6},{9,8},{10,9},{11,10},{13,12},{... | collective-permute-start | bytes 55304 | tf_op jit(solution)/shard_map/ppermute | solution.py:30
  359.4 24.6 %copy-start.41 = (f32[8,32,128]{2,1,0:T(8,128)S(1)}, f32[8,32,128]{2,1,0:T(8,128)}, u32[]{:S(2)}) copy-start(f32[8,32,128]{2,1,0:T(8,128)} %add_add_fusion.2) | copy-start | bytes 393220
  366.2 17.9 %copy-start.16 = (f32[16,64,256]{2,1,0:T(8,128)}, f32[16,64,256]{2,1,0:T(8,128)S(1)}, u32[]{:S(2)}) copy-start(f32[16,64,256]{2,1,0:T(8,128)S(1)} %fusion.65) | copy-start | bytes 3145732
  366.3 17.8 %collective-permute-start.9 = (f32[1,64,256]{2,1,0:T(8,128)S(1)}, f32[1,64,256]{2,1,0:T(8,128)S(1)}, u32[]{:S(2)}, u32[]{:S(2)}) collective-permute-start(f32[1,64,256]{2,1,0:T(8,128)S(1)} %get-tuple-element.32), channel_id=1, source_target_pairs={{0,4},{4,8},{8,12},{12,16},{16,20},{20,24},{24,28},{28,32},{32,36}... | collective-permute-start | bytes 196616 | tf_op jit(solution)/shard_map/ppermute | solution.py:28
  368.2 15.9 %collective-permute-start.8 = (f32[1,64,256]{2,1,0:T(8,128)S(1)}, f32[1,64,256]{2,1,0:T(8,128)S(1)}, u32[]{:S(2)}, u32[]{:S(2)}) collective-permute-start(f32[1,64,256]{2,1,0:T(8,128)S(1)} %get-tuple-element.33), channel_id=1, source_target_pairs={{4,0},{8,4},{12,8},{16,12},{20,16},{24,20},{28,24},{32,28},{36,32}... | collective-permute-start | bytes 196616 | tf_op jit(solution)/shard_map/ppermute | solution.py:30
  384.1 17.7 %collective-permute-start.11 = (f32[18,1,256]{2,1,0:T(1,128)S(1)}, f32[18,1,256]{2,1,0:T(1,128)S(1)}, u32[]{:S(2)}, u32[]{:S(2)}) collective-permute-start(f32[18,1,256]{2,1,0:T(1,128)S(1)} %get-tuple-element.20), channel_id=1, source_target_pairs={{0,1},{1,2},{2,3},{4,5},{5,6},{6,7},{8,9},{9,10},{10,11},{12,13},{... | collective-permute-start | bytes 55304 | tf_op jit(solution)/shard_map/ppermute | solution.py:28
  388.2 13.7 %collective-permute-start.10 = (f32[18,1,256]{2,1,0:T(1,128)S(1)}, f32[18,1,256]{2,1,0:T(1,128)S(1)}, u32[]{:S(2)}, u32[]{:S(2)}) collective-permute-start(f32[18,1,256]{2,1,0:T(1,128)S(1)} %get-tuple-element.21), channel_id=1, source_target_pairs={{1,0},{2,1},{3,2},{5,4},{6,5},{7,6},{9,8},{10,9},{11,10},{13,12},{... | collective-permute-start | bytes 55304 | tf_op jit(solution)/shard_map/ppermute | solution.py:30
  511.6 17.3 %copy-start.34 = (f32[8,128,128]{2,0,1:T(8,128)}, f32[8,128,128]{2,0,1:T(8,128)S(1)}, u32[]{:S(2)}) copy-start(f32[8,128,128]{2,0,1:T(8,128)S(1)} %broadcast_multiply_fusion.1) | copy-start | bytes 1572868
  511.6 16.5 %copy-start.15 = (f32[8,128,128]{2,0,1:T(8,128)S(1)}, f32[8,128,128]{2,0,1:T(8,128)}, u32[]{:S(2)}) copy-start(f32[8,128,128]{2,0,1:T(8,128)} %all_gather.25) | copy-start | bytes 1572868
  511.6 16.5 %copy-start.17 = (f32[8,128,128]{2,0,1:T(8,128)S(1)}, f32[8,128,128]{2,0,1:T(8,128)}, u32[]{:S(2)}) copy-start(f32[8,128,128]{2,0,1:T(8,128)} %all_gather.31) | copy-start | bytes 1572868
  511.6 16.5 %copy-start.19 = (f32[8,128,128]{2,0,1:T(8,128)S(1)}, f32[8,128,128]{2,0,1:T(8,128)}, u32[]{:S(2)}) copy-start(f32[8,128,128]{2,0,1:T(8,128)} %all_gather.30) | copy-start | bytes 1572868
  511.7 16.5 %copy-start.21 = (f32[8,128,128]{2,0,1:T(8,128)S(1)}, f32[8,128,128]{2,0,1:T(8,128)}, u32[]{:S(2)}) copy-start(f32[8,128,128]{2,0,1:T(8,128)} %all_gather.29) | copy-start | bytes 1572868
  511.7 16.5 %copy-start.23 = (f32[8,128,128]{2,0,1:T(8,128)S(1)}, f32[8,128,128]{2,0,1:T(8,128)}, u32[]{:S(2)}) copy-start(f32[8,128,128]{2,0,1:T(8,128)} %all_gather.28) | copy-start | bytes 1572868
  511.7 16.5 %copy-start.25 = (f32[8,128,128]{2,0,1:T(8,128)S(1)}, f32[8,128,128]{2,0,1:T(8,128)}, u32[]{:S(2)}) copy-start(f32[8,128,128]{2,0,1:T(8,128)} %all_gather.27) | copy-start | bytes 1572868
  511.8 15.2 %collective-permute-start.12 = (f32[1,128,128]{2,1,0:T(8,128)S(1)}, f32[1,128,128]{2,1,0:T(8,128)S(1)}, u32[]{:S(2)}, u32[]{:S(2)}) collective-permute-start(f32[1,128,128]{2,1,0:T(8,128)S(1)} %bitcast.62), channel_id=1, source_target_pairs={{4,0},{8,4},{12,8},{16,12},{20,16},{24,20},{28,24},{32,28},{36,32}... | collective-permute-start | bytes 196616 | tf_op jit(solution)/shard_map/ppermute | solution.py:30
  514.0 13.0 %collective-permute-start.13 = (f32[1,128,128]{2,1,0:T(8,128)S(1)}, f32[1,128,128]{2,1,0:T(8,128)S(1)}, u32[]{:S(2)}, u32[]{:S(2)}) collective-permute-start(f32[1,128,128]{2,1,0:T(8,128)S(1)} %bitcast.58), channel_id=1, source_target_pairs={{0,4},{4,8},{8,12},{12,16},{16,20},{20,24},{24,28},{28,32},{32,36}... | collective-permute-start | bytes 196616 | tf_op jit(solution)/shard_map/ppermute | solution.py:28
  526.9 49.1 %copy-start.27 = (f32[8,128,128]{2,0,1:T(8,128)}, f32[8,128,128]{2,0,1:T(8,128)S(1)}, u32[]{:S(2)}) copy-start(f32[8,128,128]{2,0,1:T(8,128)S(1)} %all_gather.26) | copy-start | bytes 1572868
  528.9 14.3 %copy-start.37 = (f32[8,128,128]{2,0,1:T(8,128)}, f32[8,128,128]{2,0,1:T(8,128)S(1)}, u32[]{:S(2)}) copy-start(f32[8,128,128]{2,0,1:T(8,128)S(1)} %get-tuple-element.7) | copy-start | bytes 1572868
  528.9 27.5 %copy-start.32 = (f32[8,128,128]{2,0,1:T(8,128)}, f32[8,128,128]{2,0,1:T(8,128)S(1)}, u32[]{:S(2)}) copy-start(f32[8,128,128]{2,0,1:T(8,128)S(1)} %get-tuple-element.6) | copy-start | bytes 1572868
  529.0 6.1 collective-permute-start.14
  533.2 8.0 %collective-permute-start.15 = (f32[1,128,128]{2,1,0:T(8,128)S(1)}, f32[1,128,128]{2,1,0:T(8,128)S(1)}, u32[]{:S(2)}, u32[]{:S(2)}) collective-permute-start(f32[1,128,128]{2,1,0:T(8,128)S(1)} %bitcast.59), channel_id=1, source_target_pairs={{0,4},{4,8},{8,12},{12,16},{16,20},{20,24},{24,28},{28,32},{32,36}... | collective-permute-start | bytes 196616 | tf_op jit(solution)/shard_map/ppermute | solution.py:28
  535.1 8.1 %copy-start.39 = (f32[1,128,128]{2,1,0:T(8,128)}, f32[1,128,128]{2,1,0:T(8,128)S(1)}, u32[]{:S(2)}) copy-start(f32[1,128,128]{2,1,0:T(8,128)S(1)} %collective-permute-done.14) | copy-start | bytes 196612
  543.2 34.5 %copy-start.31 = (f32[8,128,128]{2,0,1:T(8,128)}, f32[8,128,128]{2,0,1:T(8,128)S(1)}, u32[]{:S(2)}) copy-start(f32[8,128,128]{2,0,1:T(8,128)S(1)} %multiply_add_fusion.2) | copy-start | bytes 1572868
  543.3 5.5 collective-permute-start.16
  545.2 8.0 %collective-permute-start.17 = (f32[1,128,128]{2,1,0:T(8,128)S(1)}, f32[1,128,128]{2,1,0:T(8,128)S(1)}, u32[]{:S(2)}, u32[]{:S(2)}) collective-permute-start(f32[1,128,128]{2,1,0:T(8,128)S(1)} %bitcast.60), channel_id=1, source_target_pairs={{0,4},{4,8},{8,12},{12,16},{16,20},{20,24},{24,28},{28,32},{32,36}... | collective-permute-start | bytes 196616 | tf_op jit(solution)/shard_map/ppermute | solution.py:28
  562.5 13.5 %copy-start.35 = (f32[8,128,128]{2,0,1:T(8,128)S(1)}, f32[8,128,128]{2,0,1:T(8,128)}, u32[]{:S(2)}) copy-start(f32[8,128,128]{2,0,1:T(8,128)} %get-tuple-element.4) | copy-start | bytes 1572868
  562.5 13.6 %copy-start.36 = (f32[8,128,128]{2,0,1:T(8,128)S(1)}, f32[8,128,128]{2,0,1:T(8,128)}, u32[]{:S(2)}) copy-start(f32[8,128,128]{2,0,1:T(8,128)} %get-tuple-element.5) | copy-start | bytes 1572868
  563.9 5.3 collective-permute-start.18
  565.9 8.0 %collective-permute-start.19 = (f32[1,128,128]{2,1,0:T(8,128)S(1)}, f32[1,128,128]{2,1,0:T(8,128)S(1)}, u32[]{:S(2)}, u32[]{:S(2)}) collective-permute-start(f32[1,128,128]{2,1,0:T(8,128)S(1)} %bitcast.61), channel_id=1, source_target_pairs={{0,4},{4,8},{8,12},{12,16},{16,20},{20,24},{24,28},{28,32},{32,36}... | collective-permute-start | bytes 196616 | tf_op jit(solution)/shard_map/ppermute | solution.py:28
  578.8 5.4 collective-permute-start.20
  580.7 8.0 %collective-permute-start.21 = (f32[1,128,128]{2,1,0:T(8,128)S(1)}, f32[1,128,128]{2,1,0:T(8,128)S(1)}, u32[]{:S(2)}, u32[]{:S(2)}) collective-permute-start(f32[1,128,128]{2,1,0:T(8,128)S(1)} %bitcast.56), channel_id=1, source_target_pairs={{0,4},{4,8},{8,12},{12,16},{16,20},{20,24},{24,28},{28,32},{32,36}... | collective-permute-start | bytes 196616 | tf_op jit(solution)/shard_map/ppermute | solution.py:28
  584.1 6.8 copy-start.18
  584.1 6.8 copy-start.20
  584.1 6.8 copy-start.22
  584.1 6.8 copy-start.24
  663.2 29.6 %copy-start.14 = (f32[16,64,256]{2,1,0:T(8,128)S(1)}, f32[16,64,256]{2,1,0:T(8,128)}, u32[]{:S(2)}) copy-start(f32[16,64,256]{2,1,0:T(8,128)} %get-tuple-element.12) | copy-start | bytes 3145732
  665.0 8.6 %collective-permute-start.23 = (f32[1,64,256]{2,1,0:T(8,128)S(1)}, f32[1,64,256]{2,1,0:T(8,128)S(1)}, u32[]{:S(2)}, u32[]{:S(2)}) collective-permute-start(f32[1,64,256]{2,1,0:T(8,128)S(1)} %get-tuple-element.30), channel_id=1, source_target_pairs={{0,4},{4,8},{8,12},{12,16},{16,20},{20,24},{24,28},{28,32},{32,36}... | collective-permute-start | bytes 196616 | tf_op jit(solution)/shard_map/ppermute | solution.py:28
  666.9 25.9 %copy-start.5 = (f32[16,64,256]{2,1,0:T(8,128)S(1)}, f32[16,64,256]{2,1,0:T(8,128)}, u32[]{:S(2)}) copy-start(f32[16,64,256]{2,1,0:T(8,128)} %param.2) | copy-start | bytes 3145732
  666.9 25.9 %copy-start.8 = (f32[16,64,256]{2,1,0:T(8,128)S(1)}, f32[16,64,256]{2,1,0:T(8,128)}, u32[]{:S(2)}) copy-start(f32[16,64,256]{2,1,0:T(8,128)} %get-tuple-element.9) | copy-start | bytes 3145732
  666.9 25.9 %copy-start.12 = (f32[16,64,256]{2,1,0:T(8,128)S(1)}, f32[16,64,256]{2,1,0:T(8,128)}, u32[]{:S(2)}) copy-start(f32[16,64,256]{2,1,0:T(8,128)} %get-tuple-element.10) | copy-start | bytes 3145732
  666.9 25.9 %copy-start.13 = (f32[16,64,256]{2,1,0:T(8,128)S(1)}, f32[16,64,256]{2,1,0:T(8,128)}, u32[]{:S(2)}) copy-start(f32[16,64,256]{2,1,0:T(8,128)} %get-tuple-element.11) | copy-start | bytes 3145732
  666.9 8.0 %collective-permute-start.22 = (f32[1,64,256]{2,1,0:T(8,128)S(1)}, f32[1,64,256]{2,1,0:T(8,128)S(1)}, u32[]{:S(2)}, u32[]{:S(2)}) collective-permute-start(f32[1,64,256]{2,1,0:T(8,128)S(1)} %get-tuple-element.31), channel_id=1, source_target_pairs={{4,0},{8,4},{12,8},{16,12},{20,16},{24,20},{28,24},{32,28},{36,32}... | collective-permute-start | bytes 196616 | tf_op jit(solution)/shard_map/ppermute | solution.py:30
  674.9 12.4 %collective-permute-start.25 = (f32[18,1,256]{2,1,0:T(1,128)S(1)}, f32[18,1,256]{2,1,0:T(1,128)S(1)}, u32[]{:S(2)}, u32[]{:S(2)}) collective-permute-start(f32[18,1,256]{2,1,0:T(1,128)S(1)} %get-tuple-element.18), channel_id=1, source_target_pairs={{0,1},{1,2},{2,3},{4,5},{5,6},{6,7},{8,9},{9,10},{10,11},{12,13},{... | collective-permute-start | bytes 55304 | tf_op jit(solution)/shard_map/ppermute | solution.py:28
  685.4 6.6 collective-permute-start.24
  696.4 8.3 %collective-permute-start.27 = (f32[1,64,256]{2,1,0:T(8,128)S(1)}, f32[1,64,256]{2,1,0:T(8,128)S(1)}, u32[]{:S(2)}, u32[]{:S(2)}) collective-permute-start(f32[1,64,256]{2,1,0:T(8,128)S(1)} %get-tuple-element.28), channel_id=1, source_target_pairs={{0,4},{4,8},{8,12},{12,16},{16,20},{20,24},{24,28},{28,32},{32,36}... | collective-permute-start | bytes 196616 | tf_op jit(solution)/shard_map/ppermute | solution.py:28
  698.3 7.7 %collective-permute-start.26 = (f32[1,64,256]{2,1,0:T(8,128)S(1)}, f32[1,64,256]{2,1,0:T(8,128)S(1)}, u32[]{:S(2)}, u32[]{:S(2)}) collective-permute-start(f32[1,64,256]{2,1,0:T(8,128)S(1)} %get-tuple-element.29), channel_id=1, source_target_pairs={{4,0},{8,4},{12,8},{16,12},{20,16},{24,20},{28,24},{32,28},{36,32}... | collective-permute-start | bytes 196616 | tf_op jit(solution)/shard_map/ppermute | solution.py:30
  706.0 5.6 collective-permute-start.29
  709.7 6.6 collective-permute-start.28
  720.6 20.5 %copy-start.28 = (f32[16,64,256]{2,1,0:T(8,128)}, f32[16,64,256]{2,1,0:T(8,128)S(1)}, u32[]{:S(2)}) copy-start(f32[16,64,256]{2,1,0:T(8,128)S(1)} %fusion.26) | copy-start | bytes 3145732
  720.6 8.3 %collective-permute-start.31 = (f32[1,64,256]{2,1,0:T(8,128)S(1)}, f32[1,64,256]{2,1,0:T(8,128)S(1)}, u32[]{:S(2)}, u32[]{:S(2)}) collective-permute-start(f32[1,64,256]{2,1,0:T(8,128)S(1)} %get-tuple-element.26), channel_id=1, source_target_pairs={{0,4},{4,8},{8,12},{12,16},{16,20},{20,24},{24,28},{28,32},{32,36}... | collective-permute-start | bytes 196616 | tf_op jit(solution)/shard_map/ppermute | solution.py:28
  722.6 7.7 %collective-permute-start.30 = (f32[1,64,256]{2,1,0:T(8,128)S(1)}, f32[1,64,256]{2,1,0:T(8,128)S(1)}, u32[]{:S(2)}, u32[]{:S(2)}) collective-permute-start(f32[1,64,256]{2,1,0:T(8,128)S(1)} %get-tuple-element.27), channel_id=1, source_target_pairs={{4,0},{8,4},{12,8},{16,12},{20,16},{24,20},{28,24},{32,28},{36,32}... | collective-permute-start | bytes 196616 | tf_op jit(solution)/shard_map/ppermute | solution.py:30
  730.3 5.3 collective-permute-start.33
  733.7 6.6 collective-permute-start.32
  (14 other events, 32.6 us)
where the time goes:
time: 758 us; the launch traced here: 746 us
  local copies, waits for them, and re-layouts  294 us (39%)
  other arithmetic  147 us (19%)
  blocking collectives  141 us (19%)
  starting transfers between devices  122 us (16%)
  waiting for transfers between devices  38.9 us (5%)
    reshape x2, local copies, waits for them, and re-layouts, collapse_all(): array.reshape(extent[0] // 2, 2, extent[1] // 2, 2, extent[2] // 2, 2)  138 us
    psum x1, blocking collectives, per_device(): total = lax.psum(jnp.sum(source), ('space', 'group'))  66.2 us
    ppermute x17, starting transfers between devices, with_halo(): lax.ppermute(head, axis, [((i + 1) % count, i) for i in range(ends)])  61.1 us
    ppermute x17, starting transfers between devices, with_halo(): lax.ppermute(tail, axis, [(i, (i + 1) % count) for i in range(ends)])  60.5 us
    reshape x1, local copies, waits for them, and re-layouts, expand_blocks(): return spread.reshape(2 * extent[0], 2 * extent[1], 2 * extent[2])  47.4 us
    reduce_sum x2, other arithmetic, collapse_all(): array.reshape(extent[0] // 2, 2, extent[1] // 2, 2, extent[2] // 2, 2)  42.2 us
    reduce_sum x2, other arithmetic, collapse_x(): array.reshape(extent[0], extent[1] // 2, 2, extent[2] // 2, 2)  21.8 us
    broadcast_in_dim x1, local copies, waits for them, and re-layouts, expand_blocks(): jnp.broadcast_to(coarse[:, None, :, None, :, None], (extent[0], 2, extent...  21.5 us
  transfers between devices with their start and end apart: 34, of which 11 were waited for; matrix products, arithmetic and copies ran while one was open for 21% of the time, Pallas kernels for 0%

commit v1 on v0

v1 whole, which is shorter than its diff:
```python
import functools
import math

import jax
import jax.numpy as jnp
from jax import lax
from jax.experimental import pallas as pl
from jax.experimental.pallas import tpu as pltpu
from jax.sharding import PartitionSpec as P

CHEB = 6
PHASES = 8
REACTION = 0.01
RELAX = 0.8
LOWER = 0.05
UPPER = 2.0

F32 = jnp.float32
MESH = pl.DeviceIdType.MESH

PX, PY, LANES = 16, 64, 128
X0, Y0 = 4, 8
FX, FY = PX + 2 * X0, PY + 2 * Y0
W = 3
R0, RN = 4, 72
CX, CY = PX // 2, PY // 2
CW, CX0, CY0 = 7, 7, 8
GX, GY = CX + 2 * CX0, CY + 2 * CY0
DIRS = [(-1, 0), (1, 0), (0, -1), (0, 1), (-1, -1), (-1, 1), (1, -1), (1, 1)]
NO_CELL = 1 << 20


def spans(step, start, size, width):
    if step == 0:
        return pl.ds(start, size), pl.ds(start, size)
    if step > 0:
        return pl.ds(start + size - width, width), pl.ds(start - width, width)
    return pl.ds(start, width), pl.ds(start + size, width)


def fine_spans(dx, dy, wx, wy):
    return spans(dx, X0, PX, wx), spans(dy, Y0, PY, wy)


def coarse_spans(dx, dy):
    return spans(dx, CX0, CX, CW), spans(dy, CY0, CY, CY0)


def harmonic(left, right):
    return 2.0 * left * right / jnp.maximum(left + right, 1e-30)


def pieces(x):
    high = x.astype(jnp.bfloat16)
    rest = x - high.astype(F32)
    mid = rest.astype(jnp.bfloat16)
    low = (rest - mid.astype(F32)).astype(jnp.bfloat16)
    return high, mid, low


def zdot(x, matrix):
    high, mid, low = pieces(x)
    dot = functools.partial(jnp.dot, preferred_element_type=F32)
    return dot(high, matrix) + dot(mid, matrix) + dot(low, matrix)


def kernel(
    ns, ng, source_hbm, phases_hbm, out_p, out_r,
    ph, src, kap, wx, wy, wz, dg, di, fo, pa, pb, pc, res,
    cw, rem, cinv, ha, hb, cor, zbuf, ybuf, ebuf,
    part, sum1, sum2,
    in_sem, out_sem, psend, precv, send, recv,
):
    s, g = lax.axis_index("space"), lax.axis_index("group")
    lane = lax.broadcasted_iota(jnp.int32, (1, LANES), 1)

    def here(dx, dy):
        ok = jnp.bool_(True)
        if dx < 0:
            ok = s > 0
        if dx > 0:
            ok = s < ns - 1
        if dy < 0:
            ok = jnp.logical_and(ok, g > 0)
        if dy > 0:
            ok = jnp.logical_and(ok, g < ng - 1)
        return ok

    def halves(hbm, ref, sem):
        return [
            pltpu.make_async_copy(
                hbm.at[:, :, pl.ds(h * LANES, LANES)],
                ref.at[h, pl.ds(X0, PX), pl.ds(Y0, PY)],
                sem.at[h],
            )
            for h in range(2)
        ]

    load_ph = halves(phases_hbm, ph, in_sem.at[0])
    load_src = halves(source_hbm, src, in_sem.at[1])
    for copy in load_ph + load_src:
        copy.start()

    x4, q = lax.rem(s, 4), s // 4
    nq = ns // 4
    n1 = 4 * ng
    me1 = x4 * ng + g

    def peer1(j):
        t = lax.rem(me1 + j, n1)
        return (q * 4 + t // ng, lax.rem(t, ng))

    def peer2(j):
        return (lax.rem(q + j, nq) * 4 + x4, g)

    barrier = pltpu.get_barrier_semaphore()
    expected = jnp.int32(n1 - 1 + nq - 1)

    def greet(peer):
        pl.semaphore_signal(barrier, inc=1, device_id=peer, device_id_type=MESH)

    for dx, dy in DIRS:
        ok = here(dx, dy)

        @pl.when(ok)
        def _():
            greet((s + dx, g + dy))

        expected = expected + ok.astype(jnp.int32)
    for j in range(1, n1):
        greet(peer1(j))
    for j in range(1, nq):
        greet(peer2(j))

    for dx, dy in DIRS:

        @pl.when(jnp.logical_not(here(-dx, -dy)))
        def _():
            (_, tx), (_, ty) = fine_spans(dx, dy, W, Y0)
            (_, ux), (_, uy) = coarse_spans(dx, dy)
            shape = ph[:, tx, ty].shape
            ph[:, tx, ty] = jnp.full(shape, NO_CELL, jnp.int32)
            src[:, tx, ty] = jnp.zeros(shape, F32)
            pc[:, tx, ty] = jnp.zeros(shape, F32)
            cw[:, ux, uy] = jnp.zeros(cw[:, ux, uy].shape, F32)
            rem[ux, uy] = jnp.zeros(rem[ux, uy].shape, F32)

    def exchange(stage, src_at, dst_at):
        def copy(k, dx, dy):
            return pltpu.make_async_remote_copy(
                src_ref=src_at(dx, dy),
                dst_ref=dst_at(dx, dy),
                send_sem=send.at[stage, k],
                recv_sem=recv.at[stage, k],
                device_id=(s + dx, g + dy),
                device_id_type=MESH,
            )

        def start():
            for k, (dx, dy) in enumerate(DIRS):

                @pl.when(here(dx, dy))
                def _():
                    copy(k, dx, dy).start()

        def wait_recv():
            for k, (dx, dy) in enumerate(DIRS):

                @pl.when(here(-dx, -dy))
                def _():
                    copy(k, dx, dy).wait_recv()

        def wait_send():
            for k, (dx, dy) in enumerate(DIRS):

                @pl.when(here(dx, dy))
                def _():
                    copy(k, dx, dy).wait_send()

        return start, wait_recv, wait_send

    def fine_exchange(stage, a, b, width):
        def src_at(dx, dy):
            (sx, _), (sy, _) = fine_spans(dx, dy, width, width)
            return a.at[:, sx, sy]

        def dst_at(dx, dy):
            (_, tx), (_, ty) = fine_spans(dx, dy, width, width)
            return b.at[:, tx, ty]

        return exchange(stage, src_at, dst_at)

    def coarse_exchange(stage, a, lead):
        def src_at(dx, dy):
            (sx, _), (sy, _) = coarse_spans(dx, dy)
            return a.at[:, sx, sy] if lead else a.at[sx, sy]

        def dst_at(dx, dy):
            (_, tx), (_, ty) = coarse_spans(dx, dy)
            return a.at[:, tx, ty] if lead else a.at[tx, ty]

        return exchange(stage, src_at, dst_at)

    ph_start, ph_recv, ph_sent = fine_exchange(0, ph, ph, W)
    src_start, src_recv, src_sent = fine_exchange(1, src, src, W - 1)
    cw_start, cw_recv, cw_sent = coarse_exchange(2, cw, True)
    rem_start, rem_recv, rem_sent = coarse_exchange(3, rem, False)
    p_start, p_recv, p_sent = fine_exchange(4, pb, pc, W)

    for copy in load_src:
        copy.wait()

    def add_plane(x, total):
        plane = src[0, x, pl.ds(Y0, PY)] + src[1, x, pl.ds(Y0, PY)]
        return total + jnp.sum(plane.reshape(PY // 8, 8, LANES), axis=0)

    local = lax.fori_loop(X0, X0 + PX, add_plane, jnp.zeros((8, LANES), F32))
    local = jnp.sum(local, axis=0, keepdims=True)
    part[0] = local
    sum1[me1] = local
    for copy in load_ph:
        copy.wait()

    pl.semaphore_wait(barrier, expected)

    def gather_part(stage, slots, count, me, peer):
        def start():
            for j in range(1, count):
                pltpu.make_async_remote_copy(
                    src_ref=part.at[stage],
                    dst_ref=slots.at[me],
                    send_sem=psend.at[stage],
                    recv_sem=precv.at[stage],
                    device_id=peer(j),
                    device_id_type=MESH,
                ).start()

        def wait():
            pltpu.make_async_remote_copy(
                src_ref=slots.at[pl.ds(0, count - 1)],
                dst_ref=slots.at[pl.ds(0, count - 1)],
                send_sem=psend.at[stage],
                recv_sem=precv.at[stage],
                device_id=peer(1),
                device_id_type=MESH,
            ).wait()

        return start, wait

    start1, wait1 = gather_part(0, sum1, n1, me1, peer1)
    start2, wait2 = gather_part(1, sum2, nq, q, peer2)
    start1()
    ph_start()
    src_start()

    def conductivity(x, r0, n):
        for h in range(2):
            kap[h, x, pl.ds(r0, n)] = jnp.exp(
                ph[h, x, pl.ds(r0, n)].astype(F32) * (-6.0 * math.log(10.0) / (PHASES - 1))
            )

    def faces(x, r0, n):
        rows, above = pl.ds(r0, n), pl.ds(r0 + 1, n)
        k = [kap[h, x, rows] for h in range(2)]
        up = [pltpu.roll(k[h], LANES - 1, 1) for h in range(2)]
        last = lane == LANES - 1
        beside = [jnp.where(last, up[1], up[0]), jnp.where(last, 0.0, up[1])]
        for h in range(2):
            wx[h, x, rows] = harmonic(k[h], kap[h, x + 1, rows])
            wy[h, x, rows] = harmonic(k[h], kap[h, x, above])
            wz[h, x, rows] = harmonic(k[h], beside[h])

    def diagonal(x, r0, n):
        rows, below = pl.ds(r0, n), pl.ds(r0 - 1, n)
        z = [wz[h, x, rows] for h in range(2)]
        down = [pltpu.roll(z[h], 1, 1) for h in range(2)]
        first = lane == 0
        beside = [jnp.where(first, 0.0, down[0]), jnp.where(first, down[0], down[1])]
        for h in range(2):
            d = REACTION * kap[h, x, rows] + wx[h, x, rows] + wx[h, x - 1, rows]
            d = d + wy[h, x, rows] + wy[h, x, below] + z[h] + beside[h]
            dg[h, x, rows] = d
            di[h, x, rows] = jnp.where(d > 0.0, RELAX / jnp.where(d > 0.0, d, 1.0), 0.0)

    def planes(lo, hi, body):
        def step(x, carry):
            body(x)
            return carry

        lax.fori_loop(lo, hi, step, 0)

    planes(X0, X0 + PX, lambda x: conductivity(x, Y0, PY))

    def inner(x):
        faces(x, Y0, PY)

    planes(X0, X0 + PX - 1, inner)

    wait1()
    total1 = jnp.sum(sum1[...], axis=0)
    part[1] = total1
    sum2[q] = total1
    start2()

    planes(X0 + 1, X0 + PX - 1, lambda x: diagonal(x, Y0, PY))

    ph_recv()

    def halo_conductivity(x):
        conductivity(x, 0, 8)
        conductivity(x, FY - 8, 8)

    planes(X0, X0 + PX, halo_conductivity)
    for lo in (X0 - W, X0 + PX):
        planes(lo, lo + W, lambda x: conductivity(x, 0, FY))
    for lo, hi in ((X0 - W, X0 + 1), (X0 + PX - 1, X0 + PX + W - 1)):
        planes(lo, hi, lambda x: faces(x, R0, RN))

    def edge_faces(x):
        faces(x, R0, 8)
        faces(x, R0 + RN - 8, 8)

    planes(X0 + 1, X0 + PX - 1, edge_faces)
    for lo, hi in ((X0 - W + 1, X0 + 1), (X0 + PX - 1, X0 + PX + W - 1)):
        planes(lo, hi, lambda x: diagonal(x, R0, RN))

    def edge_diagonal(x):
        diagonal(x, R0, 8)
        diagonal(x, R0 + RN - 8, 8)

    planes(X0 + 1, X0 + PX - 1, edge_diagonal)

    z_in = lax.broadcasted_iota(jnp.int32, (2 * LANES, LANES), 0)
    z_out = lax.broadcasted_iota(jnp.int32, (2 * LANES, LANES), 1)
    both = jnp.where(z_in // 2 == z_out, 1.0, 0.0).astype(jnp.bfloat16)
    upper = jnp.where(z_in == 2 * z_out + 1, 1.0, 0.0).astype(jnp.bfloat16)
    outer = jnp.where(z_in == 2 * z_out + 1, 1.0, 0.0) + jnp.where(z_in == 2 * z_out - 1, 1.0, 0.0)
    outer = outer.astype(jnp.bfloat16)

    even, odd = pl.ds(Y0, CY, stride=2), pl.ds(Y0 + 1, CY, stride=2)
    under = pl.ds(Y0 - 1, CY, stride=2)

    def coarse_parts(i, carry):
        a = X0 + 2 * i
        b = a + 1
        rows = pl.ds(pl.multiple_of(i * CY, CY), CY)
        for h in range(2):
            cols = pl.ds(h * LANES, LANES)

            def pair(ref, x):
                return ref[h, x, even] + ref[h, x, odd]

            east = pair(wx, b)
            north = wy[h, a, odd] + wy[h, b, odd]
            south = wy[h, a, under] + wy[h, b, under]
            kept = REACTION * (pair(kap, a) + pair(kap, b))
            zbuf[0, rows, cols] = east
            zbuf[1, rows, cols] = north
            zbuf[2, rows, cols] = pair(wz, a) + pair(wz, b)
            zbuf[3, rows, cols] = kept + east + pair(wx, a - 1) + north + south
        return carry

    lax.fori_loop(0, CX, coarse_parts, 0)

    own = (pl.ds(CX0, CX), pl.ds(CY0, CY))
    cube = (CX, CY, LANES)
    cw[(0,) + own] = zdot(zbuf[0], both).reshape(cube)
    cw[(1,) + own] = zdot(zbuf[1], both).reshape(cube)
    cw[(2,) + own] = zdot(zbuf[2], upper).reshape(cube)
    cw[(3,) + own] = (zdot(zbuf[3], both) + zdot(zbuf[2], outer)).reshape(cube)
    cw_start()

    wait2()
    total = jnp.sum(sum2[...], axis=0)
    average = jnp.sum(total, axis=1, keepdims=True) * (1.0 / (PX * ns * PY * ng * 2 * LANES))
    src_recv()

    rows = pl.ds(R0, RN)

    def first_sweep(x):
        for h in range(2):
            f = kap[h, x, rows] * (src[h, x, rows] - average)
            fo[h, x, rows] = f
            pa[h, x, rows] = di[h, x, rows] * f

    planes(X0 - W + 1, X0 + PX + W - 1, first_sweep)

    def beside_sum(p, x, r0, n):
        mid, above, below = pl.ds(r0, n), pl.ds(r0 + 1, n), pl.ds(r0 - 1, n)
        v = [p[h, x, mid] for h in range(2)]
        z = [wz[h, x, mid] for h in range(2)]
        up = [pltpu.roll(v[h], LANES - 1, 1) for h in range(2)]
        down = [pltpu.roll(z[h] * v[h], 1, 1) for h in range(2)]
        up[0] = jnp.where(lane == LANES - 1, up[1], up[0])
        first = lane == 0
        down = [jnp.where(first, 0.0, down[0]), jnp.where(first, down[0], down[1])]
        sums = []
        for h in range(2):
            t = wx[h, x, mid] * p[h, x + 1, mid] + wx[h, x - 1, mid] * p[h, x - 1, mid]
            t = t + wy[h, x, mid] * p[h, x, above] + wy[h, x, below] * p[h, x, below]
            sums.append(t + z[h] * up[h] + down[h])
        return v, sums

    def sweep(old, new):
        def body(x):
            v, t = beside_sum(old, x, R0, RN)
            for h in range(2):
                new[h, x, rows] = (1.0 - RELAX) * v[h] + di[h, x, rows] * (fo[h, x, rows] + t[h])

        return body

    def residual(p, x):
        mid = pl.ds(Y0, PY)
        v, t = beside_sum(p, x, Y0, PY)
        return v, [fo[h, x, mid] - dg[h, x, mid] * v[h] + t[h] for h in range(2)]

    planes(X0 - 1, X0 + PX + 1, sweep(pa, pb))

    def restrict(i, carry):
        a = X0 + 2 * i
        va, ra = residual(pb, a)
        vb, rb = residual(pb, a + 1)
        dst = pl.ds(pl.multiple_of(i * CY, CY), CY)
        for h in range(2):
            pc[h, a, pl.ds(Y0, PY)] = va[h]
            pc[h, a + 1, pl.ds(Y0, PY)] = vb[h]
            ybuf[h] = ra[h] + rb[h]
            zbuf[4, dst, pl.ds(h * LANES, LANES)] = (
                ybuf[h, pl.ds(0, CY, stride=2)] + ybuf[h, pl.ds(1, CY, stride=2)]
            )
        return carry

    lax.fori_loop(0, CX, restrict, 0)
    rem[own] = zdot(zbuf[4], both).reshape(cube)
    rem_start()
    p_start()

    cw_recv()
    theta = (UPPER + LOWER) / 2.0
    delta = (UPPER - LOWER) / 2.0
    ratio = delta / theta

    def invert(x):
        r = pl.ds(1, GY - 2)
        c = cw[3, x, r]
        cinv[x, r] = jnp.where(c > 0.0, 1.0 / jnp.where(c > 0.0, c, 1.0), 0.0)

    planes(0, GX, invert)
    rem_recv()
    rem_sent()

    def first_heading(x):
        r = pl.ds(1, GY - 2)
        heading = rem[x, r] * cinv[x, r] * (1.0 / theta)
        ha[x, r] = heading
        cor[x, r] = heading

    planes(0, GX, first_heading)

    def coarse_step(old, new, r0, n, keep, add):
        mid, above, below = pl.ds(r0, n), pl.ds(r0 + 1, n), pl.ds(r0 - 1, n)

        def body(x):
            v = old[x, mid]
            u = cw[2, x, mid]
            t = cw[0, x, mid] * old[x + 1, mid] + cw[0, x - 1, mid] * old[x - 1, mid]
            t = t + cw[1, x, mid] * old[x, above] + cw[1, x, below] * old[x, below]
            t = t + u * pltpu.roll(v, LANES - 1, 1) + pltpu.roll(u * v, 1, 1)
            left = rem[x, mid] - (cw[3, x, mid] * v - t)
            rem[x, mid] = left
            heading = keep * v + add * (left * cinv[x, mid])
            new[x, mid] = heading
            cor[x, mid] = cor[x, mid] + heading

        return body

    old, new = ha, hb
    for turn in range(1, CHEB):
        following = 1.0 / (2.0 * theta / delta - ratio)
        halo = CW - turn
        n = -(-(CY + 2 * halo) // 8) * 8
        n = min(n, GY - 2 * (CY0 - halo))
        planes(
            CX0 - halo,
            CX0 + CX + halo,
            coarse_step(old, new, CY0 - halo, n, following * ratio, 2.0 * following / delta),
        )
        ratio = following
        old, new = new, old

    zi = lax.broadcasted_iota(jnp.int32, (LANES, 2 * LANES), 0)
    zo = lax.broadcasted_iota(jnp.int32, (LANES, 2 * LANES), 1)
    spread = jnp.where(zo // 2 == zi, 1.0, 0.0).astype(jnp.bfloat16)
    p_recv()

    def prolong(c):
        wide = zdot(cor[c, pl.ds(CY0 - 2, CY + 8)], spread)
        x = 2 * (c - CX0) + X0
        for h in range(2):
            part_h = wide[: CY + 4, h * LANES : (h + 1) * LANES]
            ebuf[h, pl.ds(R0, RN // 2, stride=2)] = part_h
            ebuf[h, pl.ds(R0 + 1, RN // 2, stride=2)] = part_h
            for k in range(2):
                pc[h, x + k, rows] = pc[h, x + k, rows] + ebuf[h, rows]

    planes(CX0 - 2, CX0 + CX + 2, prolong)
    planes(X0 - W + 1, X0 + PX + W - 1, sweep(pc, pa))
    p_sent()
    planes(X0 - 1, X0 + PX + 1, sweep(pa, pb))

    def stores(ref, off, hbm, sem):
        return [
            pltpu.make_async_copy(
                ref.at[h, pl.ds(off[0], PX), pl.ds(off[1], PY)],
                hbm.at[:, :, pl.ds(h * LANES, LANES)],
                sem.at[h],
            )
            for h in range(2)
        ]

    store_p = stores(pb, (X0, Y0), out_p, out_sem.at[0])
    store_r = stores(res, (0, 0), out_r, out_sem.at[1])
    for copy in store_p:
        copy.start()

    def last(x):
        _, r = residual(pb, x)
        for h in range(2):
            res[h, x - X0] = r[h]

    planes(X0, X0 + PX, last)
    for copy in store_r:
        copy.start()
    ph_sent()
    src_sent()
    cw_sent()
    for copy in store_p + store_r:
        copy.wait()


def per_device(source, phases):
    ns, ng = lax.axis_size("space"), lax.axis_size("group")
    fine = (2, FX, FY, LANES)
    coarse = (GX, GY, LANES)
    flat = CX * CY
    vmem = pltpu.VMEM
    scratch = [vmem(fine, jnp.int32)]
    scratch += [vmem(fine, F32)] * 11
    scratch += [vmem((2, PX, PY, LANES), F32), vmem((4,) + coarse, F32)]
    scratch += [vmem(coarse, F32)] * 5
    scratch += [
        vmem((5, flat, 2 * LANES), F32),
        vmem((2, PY, LANES), F32),
        vmem((2, FY, LANES), F32),
        vmem((2, 1, LANES), F32),
        vmem((4 * ng, 1, LANES), F32),
        vmem((ns // 4, 1, LANES), F32),
        pltpu.SemaphoreType.DMA((2, 2)),
        pltpu.SemaphoreType.DMA((2, 2)),
        pltpu.SemaphoreType.DMA((2,)),
        pltpu.SemaphoreType.DMA((2,)),
        pltpu.SemaphoreType.DMA((5, len(DIRS))),
        pltpu.SemaphoreType.DMA((5, len(DIRS))),
    ]
    return pl.pallas_call(
        functools.partial(kernel, ns, ng),
        out_shape=[jax.ShapeDtypeStruct(source.shape, F32)] * 2,
        in_specs=[pl.BlockSpec(memory_space=pl.ANY)] * 2,
        out_specs=[pl.BlockSpec(memory_space=pl.ANY)] * 2,
        scratch_shapes=scratch,
        compiler_params=pltpu.CompilerParams(
            collective_id=0, has_side_effects=True, vmem_limit_bytes=56 * 2**20
        ),
    )(source, phases)


def solution(mesh):
    spec = P("space", "group", None)
    return jax.shard_map(
        per_device, mesh=mesh, in_specs=(spec, spec), out_specs=(spec, spec), check_vma=False
    )
```

time: 758 us -> 68.4 us (0.09); the launches traced: 746 us -> 68.2 us
  local copies, waits for them, and re-layouts: 294 us -> 3.36 us
  other arithmetic: 147 us -> 0 us
  blocking collectives: 141 us -> 0 us
  starting transfers between devices: 122 us -> 0 us
  Pallas kernels: 0 us -> 64.2 us
  waiting for transfers between devices: 38.9 us -> 0 us
    reshape x3 -> x0, local copies, waits for them, and re-layouts: 186 us -> none  [the longest x2 138 us: collapse_all(): array.reshape(extent[0] // 2, 2, extent[1] // 2, 2, extent[2] // 2, 2)]
    ppermute x34 -> x0, starting transfers between devices: 122 us -> none  [the longest x17 61.1 us: with_halo(): lax.ppermute(head, axis, [((i + 1) % count, i) for i in range(ends)])]
    reduce_sum x9 -> x0, other arithmetic: 76.1 us -> none  [the longest x2 42.2 us: collapse_all(): array.reshape(extent[0] // 2, 2, extent[1] // 2, 2, extent[2] // 2, 2)]
    all_gather x8 -> x0, blocking collectives: 75.3 us -> none  [the longest x1 9.6 us: per_device(): lax.all_gather(coefs[0], 'group', axis=1, tiled=True)]
    slice x21 -> x0, local copies, waits for them, and re-layouts: 68.4 us -> none  [the longest x1 19 us: coarse_operator(): lower = collapse_z(weights[5][:, :, 0::2])]
    psum x1 -> x0, blocking collectives: 66.2 us -> none  [per_device(): total = lax.psum(jnp.sum(source), ('space', 'group'))]
    pallas_call x0 -> x1, Pallas kernels: none -> 64.2 us  [per_device(): pl.pallas_call(functools.partial(kernel, ns, ng), out_shape=[jax.ShapeDty...]
    ppermute x34 -> x0, waiting for transfers between devices: 38.9 us -> none  [the longest x17 19.7 us: with_halo(): lax.ppermute(tail, axis, [(i, (i + 1) % count) for i in range(ends)])]
  transfers between devices with their start and end apart: 34 -> 0, of which waited for: 11 -> 0; matrix products, arithmetic and copies ran while one was open for 21% -> 0% of each run, Pallas kernels for 0% -> 0%
where the time goes in v1:
time: 68.4 us; the launch traced here: 68.2 us
  Pallas kernels  64.2 us (94%)
  local copies, waits for them, and re-layouts  3.36 us (5%)
    pallas_call x1, Pallas kernels, per_device(): pl.pallas_call(functools.partial(kernel, ns, ng), out_shape=[jax.ShapeDty...  64.2 us
    unnamed x4, local copies, waits for them, and re-layouts  3.36 us

profile of v1, /device:TPU:9, one launch (start us, length us, event | category | flops | bytes accessed | tf_op | source)
XLA Modules:
  0.0 68.2 jit_solution(1680393203988586916)
XLA Ops:
  0.6 64.2 %shard_map.41 = (f32[16,64,256]{2,1,0:T(8,128)}, f32[16,64,256]{2,1,0:T(8,128)}) custom-call(f32[16,64,256]{2,1,0:T(8,128)} %source_hbm.1, s32[16,64,256]{2,1,0:T(8,128)} %phases_hbm.1), custom_call_target="tpu_custom_call" | custom-call | tf_op jit(solution)/shard_map/pallas_call | solution.py:565
  64.8 0.0 copy-start
  64.8 2.4 %copy.6 = f32[16,64,256]{2,1,0:T(8,128)} copy(f32[16,64,256]{2,1,0:T(8,128)} %get-tuple-element.4) | data formatting | bytes 2097152
  67.2 0.0 copy-done
  67.2 1.0 %copy.7 = f32[16,64,256]{2,1,0:T(8,128)} copy(f32[16,64,256]{2,1,0:T(8,128)S(1)} %copy-done) | data formatting | bytes 2097152
Async XLA Ops:
  64.8 2.4 %copy-start = (f32[16,64,256]{2,1,0:T(8,128)S(1)}, f32[16,64,256]{2,1,0:T(8,128)}, u32[]{:S(2)}) copy-start(f32[16,64,256]{2,1,0:T(8,128)} %get-tuple-element.5) | copy-start | bytes 3145732

commit v2 on v1

v2 whole, which is shorter than its diff:
```python
import functools
import math

import jax
import jax.numpy as jnp
from jax import lax
from jax.experimental import pallas as pl
from jax.experimental.pallas import tpu as pltpu
from jax.sharding import PartitionSpec as P

CHEB = 6
PHASES = 8
REACTION = 0.01
RELAX = 0.8
LOWER = 0.05
UPPER = 2.0

F32 = jnp.float32
MESH = pl.DeviceIdType.MESH

PX, PY, LANES = 16, 64, 128
X0, Y0 = 4, 8
FX, FY = PX + 2 * X0, PY + 2 * Y0
W = 3
R0, RN = 4, 72
CX, CY = PX // 2, PY // 2
CW, CX0, CY0 = 7, 7, 8
GX, GY = CX + 2 * CX0, CY + 2 * CY0
DIRS = [(-1, 0), (1, 0), (0, -1), (0, 1), (-1, -1), (-1, 1), (1, -1), (1, 1)]
MESSAGES = 8 * 3 + 16 + 4 + 12
NO_CELL = 1 << 20
NEAR, NEAR_ROWS, FAR_ROWS = 3, 6, 3


def spans(step, start, size, near, far):
    if step == 0:
        return pl.ds(start, size), pl.ds(start, size)
    width = far - near
    if step > 0:
        return pl.ds(start + size - far, width), pl.ds(start - far, width)
    return pl.ds(start + near, width), pl.ds(start + size + near, width)


def harmonic(left, right):
    return 2.0 * left * right / jnp.maximum(left + right, 1e-30)


def zdot(x, matrix):
    high = x.astype(jnp.bfloat16)
    rest = x - high.astype(F32)
    mid = rest.astype(jnp.bfloat16)
    low = (rest - mid.astype(F32)).astype(jnp.bfloat16)
    dot = functools.partial(jnp.dot, preferred_element_type=F32)
    return dot(high, matrix) + dot(mid, matrix) + dot(low, matrix)


def lane_map(rows, cols, place):
    i = lax.broadcasted_iota(jnp.int32, (rows, cols), 0)
    o = lax.broadcasted_iota(jnp.int32, (rows, cols), 1)
    return jnp.where(place(i, o), 1.0, 0.0).astype(jnp.bfloat16)


def planes(lo, hi, body, k=1):
    def run(first, count):
        stores = [store for j in range(count) for store in body(first + j, j)]
        for ref, at, value in stores:
            ref[at] = value

    def step(j, carry):
        run(lo + j * k, k)
        return carry

    whole = (hi - lo) // k
    lax.fori_loop(0, whole, step, 0)
    if (hi - lo) % k:
        run(lo + whole * k, (hi - lo) % k)


def kernel(
    ns, ng, source_hbm, phases_hbm, out_p, out_r,
    ph, src, kap, wx, wy, wz, dg, di, fo, pa, pb, pc,
    cw, rem, cinv, ha, hb, cor, eb, nb, zbuf, ybuf, ebuf, wide,
    part, sum1, sum2,
    in_sem, psend, precv, send, recv,
):
    s, g = lax.axis_index("space"), lax.axis_index("group")
    lane = lax.broadcasted_iota(jnp.int32, (1, LANES), 1)
    first, last = lane == 0, lane == LANES - 1

    def here(dx, dy):
        ok = jnp.bool_(True)
        if dx < 0:
            ok = s > 0
        if dx > 0:
            ok = s < ns - 1
        if dy < 0:
            ok = jnp.logical_and(ok, g > 0)
        if dy > 0:
            ok = jnp.logical_and(ok, g < ng - 1)
        return ok

    def halves(hbm, ref, sem):
        return [
            pltpu.make_async_copy(
                hbm.at[:, :, pl.ds(h * LANES, LANES)],
                ref.at[h, pl.ds(X0, PX), pl.ds(Y0, PY)],
                sem.at[h],
            )
            for h in range(2)
        ]

    load_ph = halves(phases_hbm, ph, in_sem.at[0])
    load_src = halves(source_hbm, src, in_sem.at[1])
    for copy in load_ph + load_src:
        copy.start()

    x4, q = lax.rem(s, 4), s // 4
    nq = ns // 4
    n1 = 4 * ng
    me1 = x4 * ng + g

    def peer1(j):
        t = lax.rem(me1 + j, n1)
        return (q * 4 + t // ng, lax.rem(t, ng))

    def peer2(j):
        return (lax.rem(q + j, nq) * 4 + x4, g)

    barrier = pltpu.get_barrier_semaphore()
    expected = jnp.int32(n1 - 1 + nq - 1)

    def greet(peer):
        pl.semaphore_signal(barrier, inc=1, device_id=peer, device_id_type=MESH)

    for j in range(1, n1):
        greet(peer1(j))
    for j in range(1, nq):
        greet(peer2(j))
    for dx, dy in DIRS:
        ok = here(dx, dy)

        @pl.when(ok)
        def _():
            greet((s + dx, g + dy))

        expected = expected + ok.astype(jnp.int32)

    used = [0]

    def exchange(messages):
        base = used[0]
        used[0] += len(messages)

        def copy(k):
            (dx, dy), source, target = messages[k]
            return pltpu.make_async_remote_copy(
                src_ref=source,
                dst_ref=target,
                send_sem=send.at[base + k],
                recv_sem=recv.at[base + k],
                device_id=(s + dx, g + dy),
                device_id_type=MESH,
            )

        def each(sign, act):
            for k, ((dx, dy), _, _) in enumerate(messages):

                @pl.when(here(sign * dx, sign * dy))
                def _():
                    act(copy(k))

        return (
            lambda: each(1, lambda c: c.start()),
            lambda: each(-1, lambda c: c.wait_recv()),
            lambda: each(1, lambda c: c.wait_send()),
        )

    def fill(messages, value):
        for (dx, dy), _, target in messages:

            @pl.when(jnp.logical_not(here(-dx, -dy)))
            def _():
                target[...] = jnp.full(target.shape, value, target.dtype)

    def fine_messages(a, b, width, skip=0):
        messages = []
        for dx, dy in DIRS:
            reach = width - 1 if dx and dy else width
            sx, tx = spans(dx, X0, PX, 0 if dy else skip, reach)
            sy, ty = spans(dy, Y0, PY, 0, reach)
            messages.append(((dx, dy), a.at[:, sx, sy], b.at[:, tx, ty]))
        return messages

    def coarse_messages(a, parts):
        messages = []
        for dx, dy in DIRS:
            if dx and dy:
                boxes = [(0, NEAR, NEAR_ROWS, None), (NEAR, CW - 1, FAR_ROWS, None)]
            else:
                boxes = [(0, far, CW, span) for span, far in parts or [(None, CW)]]
            for near, far, count, span in boxes:
                sx, tx = spans(dx, CX0, CX, near, far)
                sy, ty = spans(dy, CY0, CY, 0, count)
                lead = () if parts is None else (span or slice(None),)
                messages.append(((dx, dy), a.at[lead + (sx, sy)], a.at[lead + (tx, ty)]))
        return messages

    ph_all = fine_messages(ph, ph, W)
    src_all = fine_messages(src, src, W - 1)
    p_all = fine_messages(pb, pc, W, 1)
    cw_all = coarse_messages(cw, [(pl.ds(0, 2), CW), (pl.ds(2, 2), CW - 1)])
    rem_all = coarse_messages(rem, None)
    rim_all = []
    for d in (-1, 1):
        sx, tx = spans(d, CX0, CX, 0, CW)
        sy, ty = spans(d, CY0, CY, 0, CW)
        rim_all.append(((d, 0), nb.at[sx], nb.at[tx]))
        rim_all.append(((0, d), eb.at[:, sy], eb.at[:, ty]))
    fill(fine_messages(ph, ph, W), NO_CELL)
    for messages in (src_all, p_all, cw_all, rem_all, rim_all):
        fill(messages, 0)
    ph_start, ph_recv, ph_sent = exchange(ph_all)
    src_start, src_recv, src_sent = exchange(src_all)
    cw_start, cw_recv, cw_sent = exchange(cw_all)
    rim_start, rim_recv, rim_sent = exchange(rim_all)
    rem_start, rem_recv, rem_sent = exchange(rem_all)
    p_start, p_recv, p_sent = exchange(p_all)

    def conductivity(x, r0, n):
        at = pl.ds(r0, n)
        rate = -6.0 * math.log(10.0) / (PHASES - 1)
        return [(kap, (h, x, at), jnp.exp(ph[h, x, at].astype(F32) * rate)) for h in range(2)]

    def faces(x, r0, n):
        rows, above = pl.ds(r0, n), pl.ds(r0 + 1, n)
        k = [kap[h, x, rows] for h in range(2)]
        up = [pltpu.roll(k[h], LANES - 1, 1) for h in range(2)]
        beside = [jnp.where(last, up[1], up[0]), jnp.where(last, 0.0, up[1])]
        stores = []
        for h in range(2):
            stores.append((wx, (h, x, rows), harmonic(k[h], kap[h, x + 1, rows])))
            stores.append((wy, (h, x, rows), harmonic(k[h], kap[h, x, above])))
            stores.append((wz, (h, x, rows), harmonic(k[h], beside[h])))
        return stores

    def diagonal(x, r0, n):
        rows, below = pl.ds(r0, n), pl.ds(r0 - 1, n)
        z = [wz[h, x, rows] for h in range(2)]
        down = [pltpu.roll(z[h], 1, 1) for h in range(2)]
        beside = [jnp.where(first, 0.0, down[0]), jnp.where(first, down[0], down[1])]
        stores = []
        for h in range(2):
            d = REACTION * kap[h, x, rows] + wx[h, x, rows] + wx[h, x - 1, rows]
            d = d + wy[h, x, rows] + wy[h, x, below] + z[h] + beside[h]
            stores.append((dg, (h, x, rows), d))
            scaled = jnp.where(d > 0.0, RELAX / jnp.where(d > 0.0, d, 1.0), 0.0)
            stores.append((di, (h, x, rows), scaled))
        return stores

    def zero(ref, at):
        ref[at] = jnp.zeros(ref.at[at].shape, F32)

    for copy in load_ph:
        copy.wait()
    planes(X0, X0 + PX, lambda x, _: conductivity(x, Y0, PY), 2)
    both_h = pl.ds(0, 2)
    zero(kap, (both_h, X0 + PX, pl.ds(Y0, PY)))
    zero(wx, (both_h, X0 - 1, pl.ds(Y0, PY)))
    zero(kap, (both_h, pl.ds(X0, PX), pl.ds(Y0 + PY, 8)))
    zero(wy, (both_h, pl.ds(X0, PX), pl.ds(0, Y0)))

    for copy in load_src:
        copy.wait()

    def add_plane(x, total):
        plane = src[0, x, pl.ds(Y0, PY)] + src[1, x, pl.ds(Y0, PY)]
        return total + jnp.sum(plane.reshape(PY // 8, 8, LANES), axis=0)

    local = lax.fori_loop(X0, X0 + PX, add_plane, jnp.zeros((8, LANES), F32))
    local = jnp.sum(local, axis=0, keepdims=True)
    part[0] = local
    sum1[me1] = local

    pl.semaphore_wait(barrier, expected)

    def gather_part(stage, slots, count, me, peer):
        def start():
            for j in range(1, count):
                pltpu.make_async_remote_copy(
                    src_ref=part.at[stage],
                    dst_ref=slots.at[me],
                    send_sem=psend.at[stage],
                    recv_sem=precv.at[stage],
                    device_id=peer(j),
                    device_id_type=MESH,
                ).start()

        def wait():
            pltpu.make_async_remote_copy(
                src_ref=slots.at[pl.ds(0, count - 1)],
                dst_ref=slots.at[pl.ds(0, count - 1)],
                send_sem=psend.at[stage],
                recv_sem=precv.at[stage],
                device_id=peer(1),
                device_id_type=MESH,
            ).wait()

        return start, wait

    start1, wait1 = gather_part(0, sum1, n1, me1, peer1)
    start2, wait2 = gather_part(1, sum2, nq, q, peer2)
    start1()
    ph_start()
    src_start()

    planes(X0, X0 + PX, lambda x, _: faces(x, Y0, PY), 2)

    both = lane_map(2 * LANES, LANES, lambda i, o: i // 2 == o)
    upper = lane_map(2 * LANES, LANES, lambda i, o: i == 2 * o + 1)
    outer = lane_map(2 * LANES, LANES, lambda i, o: (i == 2 * o + 1) | (i == 2 * o - 1))
    even, odd = pl.ds(Y0, CY, stride=2), pl.ds(Y0 + 1, CY, stride=2)
    under = pl.ds(Y0 - 1, CY, stride=2)

    def pair(ref, h, x):
        return ref[h, x, even] + ref[h, x, odd]

    def coarse_parts(i, _):
        a = X0 + 2 * i
        b = a + 1
        rows = pl.ds(pl.multiple_of(i * CY, CY), CY)
        stores = []
        for h in range(2):
            cols = pl.ds(h * LANES, LANES)
            east = pair(wx, h, b)
            north = wy[h, a, odd] + wy[h, b, odd]
            south = wy[h, a, under] + wy[h, b, under]
            kept = REACTION * (pair(kap, h, a) + pair(kap, h, b))
            middle = kept + east + pair(wx, h, a - 1) + north + south
            for k, value in enumerate((middle, east, north, pair(wz, h, a) + pair(wz, h, b))):
                stores.append((zbuf, (k, rows, cols), value))
        return stores

    planes(0, CX, coarse_parts, 2)

    own = (pl.ds(CX0, CX), pl.ds(CY0, CY))
    cube = (CX, CY, LANES)
    cw[(0,) + own] = (zdot(zbuf[0], both) + zdot(zbuf[3], outer)).reshape(cube)
    cw[(1,) + own] = zdot(zbuf[1], both).reshape(cube)
    cw[(2,) + own] = zdot(zbuf[2], both).reshape(cube)
    cw[(3,) + own] = zdot(zbuf[3], upper).reshape(cube)
    wait1()
    total1 = jnp.sum(sum1[...], axis=0)
    part[1] = total1
    sum2[q] = total1
    start2()

    planes(X0 + 1, X0 + PX - 1, lambda x, _: diagonal(x, Y0, PY), 2)

    ph_recv()

    def sides(body, lo, hi):
        def both_sides(x, _):
            return body(x, lo, 8) + body(x, hi, 8)

        return both_sides

    planes(X0, X0 + PX, sides(conductivity, 0, FY - 8), 4)
    for lo in (X0 - W, X0 + PX):
        planes(lo, lo + W, lambda x, _: conductivity(x, 0, FY), 3)
    for lo, hi in ((X0 - W, X0 + 1), (X0 + PX - 1, X0 + PX + W - 1)):
        planes(lo, hi, lambda x, _: faces(x, R0, RN), 2)
    planes(X0 + 1, X0 + PX - 1, sides(faces, R0, R0 + RN - 8), 7)

    zbuf[4, pl.ds(0, CY)] = jnp.concatenate([pair(wx, h, X0 - 1) for h in range(2)], axis=1)
    zbuf[4, pl.ds(CY, CY)] = jnp.concatenate([pair(wx, h, X0 + PX - 1) for h in range(2)], axis=1)
    for i in range(CX):
        for k, row in enumerate((Y0 - 1, Y0 + PY - 1)):
            for h in range(2):
                zbuf[4, pl.ds(2 * CY + k * CX + i, 1), pl.ds(h * LANES, LANES)] = (
                    wy[h, X0 + 2 * i, pl.ds(row, 1)] + wy[h, X0 + 2 * i + 1, pl.ds(row, 1)]
                )
    rim = zdot(zbuf[4, pl.ds(0, 2 * CY + 2 * CX)], both)
    eb[0, pl.ds(CY0, CY)] = rim[:CY]
    eb[1, pl.ds(CY0, CY)] = rim[CY : 2 * CY]
    for i in range(CX):
        for k in range(2):
            j = 2 * CY + k * CX + i
            nb[CX0 + i, pl.ds(k, 1)] = rim[j : j + 1]
    rim_start()

    for lo, hi in ((X0 - W + 1, X0 + 1), (X0 + PX - 1, X0 + PX + W - 1)):
        planes(lo, hi, lambda x, _: diagonal(x, R0, RN), 3)
    planes(X0 + 1, X0 + PX - 1, sides(diagonal, R0, R0 + RN - 8), 7)

    wait2()
    total = jnp.sum(sum2[...], axis=0)
    average = jnp.sum(total, axis=1, keepdims=True) * (1.0 / (PX * ns * PY * ng * 2 * LANES))
    src_recv()
    cw_start()

    rows = pl.ds(R0, RN)

    def first_sweep(x, _):
        stores = []
        for h in range(2):
            f = kap[h, x, rows] * (src[h, x, rows] - average)
            stores.append((fo, (h, x, rows), f))
            stores.append((pa, (h, x, rows), di[h, x, rows] * f))
        return stores

    planes(X0 - W + 1, X0 + PX + W - 1, first_sweep, 2)

    def beside_sum(p, x, r0, n):
        mid, above, below = pl.ds(r0, n), pl.ds(r0 + 1, n), pl.ds(r0 - 1, n)
        v = [p[h, x, mid] for h in range(2)]
        z = [wz[h, x, mid] for h in range(2)]
        up = [pltpu.roll(v[h], LANES - 1, 1) for h in range(2)]
        down = [pltpu.roll(z[h] * v[h], 1, 1) for h in range(2)]
        up[0] = jnp.where(last, up[1], up[0])
        down = [jnp.where(first, 0.0, down[0]), jnp.where(first, down[0], down[1])]
        sums = []
        for h in range(2):
            t = wx[h, x, mid] * p[h, x + 1, mid] + wx[h, x - 1, mid] * p[h, x - 1, mid]
            t = t + wy[h, x, mid] * p[h, x, above] + wy[h, x, below] * p[h, x, below]
            sums.append(t + z[h] * up[h] + down[h])
        return v, sums

    def sweep(old, new):
        def body(x, _):
            v, t = beside_sum(old, x, R0, RN)
            return [
                (new, (h, x, rows), (1.0 - RELAX) * v[h] + di[h, x, rows] * (fo[h, x, rows] + t[h]))
                for h in range(2)
            ]

        return body

    mid = pl.ds(Y0, PY)

    def residual(p, x):
        v, t = beside_sum(p, x, Y0, PY)
        return v, [fo[h, x, mid] - dg[h, x, mid] * v[h] + t[h] for h in range(2)]

    planes(X0 - 1, X0 + PX + 1, sweep(pa, pb), 2)

    def restrict(i, slot):
        a = X0 + 2 * i
        va, ra = residual(pb, a)
        vb, rb = residual(pb, a + 1)
        dst = pl.ds(pl.multiple_of(i * CY, CY), CY)
        stores = []
        for h in range(2):
            stores.append((pc, (h, a, mid), va[h]))
            stores.append((pc, (h, a + 1, mid), vb[h]))
            ybuf[slot, h] = ra[h] + rb[h]
            halves_y = ybuf[slot, h, pl.ds(0, CY, stride=2)] + ybuf[slot, h, pl.ds(1, CY, stride=2)]
            stores.append((zbuf, (4, dst, pl.ds(h * LANES, LANES)), halves_y))
        return stores

    planes(0, CX, restrict, 2)
    rem[own] = zdot(zbuf[4], both).reshape(cube)
    rem_start()
    p_start()
    for x in (X0 - 1, X0 + PX):
        pc[:, x, mid] = pb[:, x, mid]

    theta = (UPPER + LOWER) / 2.0
    delta = (UPPER - LOWER) / 2.0
    ratio = delta / theta
    cw_recv()
    cw_sent()
    rim_recv()
    body_rows = pl.ds(1, GY - 2)
    for k, x in enumerate((CX0 - 1, CX0 + CX - 1)):
        east = eb[k, body_rows]
        cw[1, x, body_rows] = east
        for j in (x, x + 1):
            cw[0, j, body_rows] = cw[0, j, body_rows] + east

    def rim_rows(x, _):
        stores = []
        for k, r in enumerate((CY0 - 1, CY0 + CY - 1)):
            north = nb[x, pl.ds(k, 1)]
            stores.append((cw, (2, x, pl.ds(r, 1)), north))
            for j in (r, r + 1):
                stores.append((cw, (0, x, pl.ds(j, 1)), cw[0, x, pl.ds(j, 1)] + north))
        return stores

    planes(0, GX, rim_rows, 2)

    def invert(x, _):
        c = cw[0, x, body_rows]
        c = jnp.where(c > 0.0, 1.0 / jnp.where(c > 0.0, c, 1.0), 0.0)
        return [(cinv, (x, body_rows), c)]

    planes(0, GX, invert, 2)
    rem_recv()
    rem_sent()

    def first_heading(x, _):
        heading = rem[x, body_rows] * cinv[x, body_rows] * (1.0 / theta)
        return [(ha, (x, body_rows), heading), (cor, (x, body_rows), heading)]

    planes(0, GX, first_heading, 2)

    def coarse_step(old, new, r0, n, keep, add):
        mid, above, below = pl.ds(r0, n), pl.ds(r0 + 1, n), pl.ds(r0 - 1, n)

        def body(x, _):
            v = old[x, mid]
            u = cw[3, x, mid]
            t = cw[1, x, mid] * old[x + 1, mid] + cw[1, x - 1, mid] * old[x - 1, mid]
            t = t + cw[2, x, mid] * old[x, above] + cw[2, x, below] * old[x, below]
            t = t + u * pltpu.roll(v, LANES - 1, 1) + pltpu.roll(u * v, 1, 1)
            left = rem[x, mid] - (cw[0, x, mid] * v - t)
            heading = keep * v + add * (left * cinv[x, mid])
            return [
                (rem, (x, mid), left),
                (new, (x, mid), heading),
                (cor, (x, mid), cor[x, mid] + heading),
            ]

        return body

    old, new = ha, hb
    for turn in range(1, CHEB):
        following = 1.0 / (2.0 * theta / delta - ratio)
        halo = CW - turn
        lo, hi = CX0 - halo, CX0 + CX + halo
        step = coarse_step(
            old, new, CY0 - halo, CY + 2 * halo, following * ratio, 2.0 * following / delta
        )
        planes(lo, hi, step, {20: 5, 18: 6, 16: 4, 14: 7, 12: 6}[hi - lo])
        ratio = following
        old, new = new, old

    spread = lane_map(LANES, 2 * LANES, lambda i, o: o // 2 == i)
    top = CX + 4
    picked = cor[pl.ds(CX0 - 2, top), pl.ds(CY0 - 2, CY + 8)]
    wide[...] = zdot(picked.reshape(top * (CY + 8), LANES), spread)
    p_recv()

    def prolong(c, slot):
        x = 2 * c + X0 - 4
        stores = []
        for h in range(2):
            part_h = wide[pl.ds(pl.multiple_of(c * (CY + 8), 8), CY + 4), pl.ds(h * LANES, LANES)]
            ebuf[slot, h, pl.ds(R0, RN // 2, stride=2)] = part_h
            ebuf[slot, h, pl.ds(R0 + 1, RN // 2, stride=2)] = part_h
            for k in range(2):
                stores.append((pc, (h, x + k, rows), pc[h, x + k, rows] + ebuf[slot, h, rows]))
        return stores

    planes(0, top, prolong, 2)
    planes(X0 - W + 1, X0 + PX + W - 1, sweep(pc, pa), 2)
    p_sent()
    planes(X0 - 1, X0 + PX + 1, sweep(pa, pb), 2)

    def finish(x, _):
        v, r = residual(pb, x)
        stores = []
        for h in range(2):
            at = (x - X0, pl.ds(0, PY), pl.ds(h * LANES, LANES))
            stores += [(out_p, at, v[h]), (out_r, at, r[h])]
        return stores

    planes(X0, X0 + PX, finish, 2)
    ph_sent()
    src_sent()
    rim_sent()


def write_out(p, r, out_p, out_r, sem):
    copies = [pltpu.make_async_copy(p, out_p, sem.at[0]), pltpu.make_async_copy(r, out_r, sem.at[1])]
    for copy in copies:
        copy.start()
    for copy in copies:
        copy.wait()


def per_device(source, phases):
    ns, ng = lax.axis_size("space"), lax.axis_size("group")
    fine = (2, FX, FY, LANES)
    coarse = (GX, GY, LANES)
    flat = CX * CY
    vmem = pltpu.VMEM
    scratch = [vmem(fine, jnp.int32)]
    scratch += [vmem(fine, F32)] * 11
    scratch += [vmem((4,) + coarse, F32)]
    scratch += [vmem(coarse, F32)] * 5
    scratch += [
        vmem((2, GY, LANES), F32),
        vmem((GX, 2, LANES), F32),
        vmem((5, flat, 2 * LANES), F32),
        vmem((2, 2, PY, LANES), F32),
        vmem((2, 2, FY, LANES), F32),
        vmem(((CX + 4) * (CY + 8), 2 * LANES), F32),
        vmem((2, 1, LANES), F32),
        vmem((4 * ng, 1, LANES), F32),
        vmem((ns // 4, 1, LANES), F32),
        pltpu.SemaphoreType.DMA((2, 2)),
        pltpu.SemaphoreType.DMA((2,)),
        pltpu.SemaphoreType.DMA((2,)),
        pltpu.SemaphoreType.DMA((MESSAGES,)),
        pltpu.SemaphoreType.DMA((MESSAGES,)),
    ]
    out_shape = [jax.ShapeDtypeStruct(source.shape, F32)] * 2
    pressure, residual = pl.pallas_call(
        functools.partial(kernel, ns, ng),
        out_shape=out_shape,
        in_specs=[pl.BlockSpec(memory_space=pltpu.HBM)] * 2,
        out_specs=[pl.BlockSpec(memory_space=pltpu.VMEM)] * 2,
        scratch_shapes=scratch,
        compiler_params=pltpu.CompilerParams(
            collective_id=0, has_side_effects=True, vmem_limit_bytes=40 * 2**20
        ),
    )(source, phases)
    return pl.pallas_call(
        write_out,
        out_shape=out_shape,
        in_specs=[pl.BlockSpec(memory_space=pl.ANY)] * 2,
        out_specs=[pl.BlockSpec(memory_space=pl.ANY)] * 2,
        scratch_shapes=[pltpu.SemaphoreType.DMA((2,))],
        compiler_params=pltpu.CompilerParams(vmem_limit_bytes=2**20),
    )(pressure, residual)


def solution(mesh):
    spec = P("space", "group", None)
    return jax.shard_map(
        per_device, mesh=mesh, in_specs=(spec, spec), out_specs=(spec, spec), check_vma=False
    )
```

time: 68.4 us -> 52.3 us (0.76)
  Pallas kernels: 64.2 us -> 48.5 us
  local copies, waits for them, and re-layouts: 3.36 us -> 2.44 us
    pallas_call x1 -> x2, Pallas kernels: 64.2 us -> 48.5 us  [the longest x1 47.2 us: per_device(): pl.pallas_call(functools.partial(kernel, ns, ng), out_shape=out_shape, in...]
    unnamed x4, local copies, waits for them, and re-layouts: 3.36 us -> 2.44 us
where the time goes in v2:
time: 52.3 us; the launch traced here: 51.6 us
  Pallas kernels  48.5 us (93%)
  local copies, waits for them, and re-layouts  2.44 us (5%)
  between operations  0.65 us (1%)
    pallas_call x1, Pallas kernels, per_device(): pl.pallas_call(functools.partial(kernel, ns, ng), out_shape=out_shape, in...  47.2 us
    unnamed x4, local copies, waits for them, and re-layouts  2.44 us
    pallas_call x1, Pallas kernels, per_device(): pl.pallas_call(write_out, out_shape=out_shape, in_specs=[pl.BlockSpec(mem...  1.33 us

profile of v2, /device:TPU:9, one launch (start us, length us, event | category | flops | bytes accessed | tf_op | source)
XLA Modules:
  0.0 51.6 jit_solution(822769764873260279)
XLA Ops:
  0.6 0.0 copy-start
  0.6 1.2 %copy-done = f32[16,64,256]{2,1,0:T(8,128)S(1)} copy-done((f32[16,64,256]{2,1,0:T(8,128)S(1)}, f32[16,64,256]{2,1,0:T(8,128)}, u32[]{:S(2)}) %copy-start) | copy-done | bytes 1048600
  1.9 0.0 copy-start.1
  1.9 1.2 %copy-done.1 = s32[16,64,256]{2,1,0:T(8,128)S(1)} copy-done((s32[16,64,256]{2,1,0:T(8,128)S(1)}, s32[16,64,256]{2,1,0:T(8,128)}, u32[]{:S(2)}) %copy-start.1) | copy-done | bytes 1048600
  3.1 47.2 %shard_map.41 = (f32[16,64,256]{2,1,0:T(8,128)S(1)}, f32[16,64,256]{2,1,0:T(8,128)S(1)}) custom-call(f32[16,64,256]{2,1,0:T(8,128)S(1)} %copy-done, s32[16,64,256]{2,1,0:T(8,128)S(1)} %copy-done.1), custom_call_target="tpu_custom_call" | custom-call | tf_op jit(solution)/shard_map/pallas_call | solution.py:608
  50.3 1.3 %shard_map.42 = (f32[16,64,256]{2,1,0:T(8,128)}, f32[16,64,256]{2,1,0:T(8,128)}) custom-call(f32[16,64,256]{2,1,0:T(8,128)S(1)} %get-tuple-element.4.p, f32[16,64,256]{2,1,0:T(8,128)S(1)} %get-tuple-element.5.r), custom_call_target="tpu_custom_call" | custom-call | tf_op jit(solution)/shard_map/pallas_call | solution.py:618
Async XLA Ops:
  0.6 1.2 %copy-start = (f32[16,64,256]{2,1,0:T(8,128)S(1)}, f32[16,64,256]{2,1,0:T(8,128)}, u32[]{:S(2)}) copy-start(f32[16,64,256]{2,1,0:T(8,128)} %source_hbm.1) | copy-start | bytes 3145732
  1.9 1.2 %copy-start.1 = (s32[16,64,256]{2,1,0:T(8,128)S(1)}, s32[16,64,256]{2,1,0:T(8,128)}, u32[]{:S(2)}) copy-start(s32[16,64,256]{2,1,0:T(8,128)} %phases_hbm.1) | copy-start | bytes 3145732

commit v3 on v2

--- a/solution.py
+++ b/solution.py
@@ -26,8 +26,9 @@
 CX, CY = PX // 2, PY // 2
 CW, CX0, CY0 = 7, 7, 8
 GX, GY = CX + 2 * CX0, CY + 2 * CY0
+CS = CY + 8
 DIRS = [(-1, 0), (1, 0), (0, -1), (0, 1), (-1, -1), (-1, 1), (1, -1), (1, 1)]
-MESSAGES = 8 * 3 + 16 + 4 + 12
+MESSAGES = 8 * 4 + 16 + 12
 NO_CELL = 1 << 20
 NEAR, NEAR_ROWS, FAR_ROWS = 3, 6, 3
 
@@ -79,7 +80,7 @@
 def kernel(
     ns, ng, source_hbm, phases_hbm, out_p, out_r,
     ph, src, kap, wx, wy, wz, dg, di, fo, pa, pb, pc,
-    cw, rem, cinv, ha, hb, cor, eb, nb, zbuf, ybuf, ebuf, wide,
+    cw, cc, rem, ha, hb, cor, near, zbuf, ybuf, ebuf, wide,
     part, sum1, sum2,
     in_sem, psend, precv, send, recv,
 ):
@@ -208,23 +209,23 @@
     ph_all = fine_messages(ph, ph, W)
     src_all = fine_messages(src, src, W - 1)
     p_all = fine_messages(pb, pc, W, 1)
-    cw_all = coarse_messages(cw, [(pl.ds(0, 2), CW), (pl.ds(2, 2), CW - 1)])
+    cw_all = coarse_messages(cw, [(pl.ds(0, 1), CW), (pl.ds(1, 2), CW - 1)])
     rem_all = coarse_messages(rem, None)
-    rim_all = []
-    for d in (-1, 1):
-        sx, tx = spans(d, CX0, CX, 0, CW)
-        sy, ty = spans(d, CY0, CY, 0, CW)
-        rim_all.append(((d, 0), nb.at[sx], nb.at[tx]))
-        rim_all.append(((0, d), eb.at[:, sy], eb.at[:, ty]))
+    near_all = []
+    for dx, dy in DIRS:
+        reach = 1 if dx and dy else 2
+        sx, tx = spans(dx, CX0, CX, 0, reach)
+        sy, ty = spans(dy, CY0, CY, 0, reach)
+        near_all.append(((dx, dy), near.at[sx, sy], near.at[tx, ty]))
     fill(fine_messages(ph, ph, W), NO_CELL)
-    for messages in (src_all, p_all, cw_all, rem_all, rim_all):
+    for messages in (src_all, p_all, cw_all, rem_all, near_all):
         fill(messages, 0)
     ph_start, ph_recv, ph_sent = exchange(ph_all)
     src_start, src_recv, src_sent = exchange(src_all)
     cw_start, cw_recv, cw_sent = exchange(cw_all)
-    rim_start, rim_recv, rim_sent = exchange(rim_all)
     rem_start, rem_recv, rem_sent = exchange(rem_all)
     p_start, p_recv, p_sent = exchange(p_all)
+    near_start, near_recv, near_sent = exchange(near_all)
 
     def conductivity(x, r0, n):
         at = pl.ds(r0, n)
@@ -257,17 +258,9 @@
             stores.append((di, (h, x, rows), scaled))
         return stores
 
-    def zero(ref, at):
-        ref[at] = jnp.zeros(ref.at[at].shape, F32)
-
     for copy in load_ph:
         copy.wait()
-    planes(X0, X0 + PX, lambda x, _: conductivity(x, Y0, PY), 2)
-    both_h = pl.ds(0, 2)
-    zero(kap, (both_h, X0 + PX, pl.ds(Y0, PY)))
-    zero(wx, (both_h, X0 - 1, pl.ds(Y0, PY)))
-    zero(kap, (both_h, pl.ds(X0, PX), pl.ds(Y0 + PY, 8)))
-    zero(wy, (both_h, pl.ds(X0, PX), pl.ds(0, Y0)))
+    planes(X0, X0 + PX, lambda x, _: conductivity(x, Y0, PY), 4)
 
     for copy in load_src:
         copy.wait()
@@ -313,13 +306,36 @@
     ph_start()
     src_start()
 
-    planes(X0, X0 + PX, lambda x, _: faces(x, Y0, PY), 2)
+    planes(X0, X0 + PX, lambda x, _: faces(x, Y0, PY), 4)
+
+    wait1()
+    total1 = jnp.sum(sum1[...], axis=0)
+    part[1] = total1
+    sum2[q] = total1
+    start2()
+
+    planes(X0 + 1, X0 + PX - 1, lambda x, _: diagonal(x, Y0, PY), 7)
+
+    ph_recv()
+
+    def sides(body, lo, hi):
+        def both_sides(x, _):
+            return body(x, lo, 8) + body(x, hi, 8)
+
+        return both_sides
+
+    planes(X0, X0 + PX, sides(conductivity, 0, FY - 8), 4)
+    for lo in (X0 - W, X0 + PX):
+        planes(lo, lo + W, lambda x, _: conductivity(x, 0, FY), 3)
+    for lo, hi in ((X0 - W, X0 + 1), (X0 + PX - 1, X0 + PX + W - 1)):
+        planes(lo, hi, lambda x, _: faces(x, R0, RN), 2)
+    planes(X0 + 1, X0 + PX - 1, sides(faces, R0, R0 + RN - 8), 7)
 
     both = lane_map(2 * LANES, LANES, lambda i, o: i // 2 == o)
     upper = lane_map(2 * LANES, LANES, lambda i, o: i == 2 * o + 1)
     outer = lane_map(2 * LANES, LANES, lambda i, o: (i == 2 * o + 1) | (i == 2 * o - 1))
-    even, odd = pl.ds(Y0, CY, stride=2), pl.ds(Y0 + 1, CY, stride=2)
-    under = pl.ds(Y0 - 1, CY, stride=2)
+    even, odd = pl.ds(Y0, CY + 1, stride=2), pl.ds(Y0 + 1, CY + 1, stride=2)
+    under = pl.ds(Y0 - 1, CY + 1, stride=2)
 
     def pair(ref, h, x):
         return ref[h, x, even] + ref[h, x, odd]
@@ -327,7 +343,7 @@
     def coarse_parts(i, _):
         a = X0 + 2 * i
         b = a + 1
-        rows = pl.ds(pl.multiple_of(i * CY, CY), CY)
+        rows = pl.ds(pl.multiple_of(i * CS, 8), CY + 1)
         stores = []
         for h in range(2):
             cols = pl.ds(h * LANES, LANES)
@@ -340,53 +356,33 @@
                 stores.append((zbuf, (k, rows, cols), value))
         return stores
 
-    planes(0, CX, coarse_parts, 2)
-
-    own = (pl.ds(CX0, CX), pl.ds(CY0, CY))
-    cube = (CX, CY, LANES)
-    cw[(0,) + own] = (zdot(zbuf[0], both) + zdot(zbuf[3], outer)).reshape(cube)
-    cw[(1,) + own] = zdot(zbuf[1], both).reshape(cube)
-    cw[(2,) + own] = zdot(zbuf[2], both).reshape(cube)
-    cw[(3,) + own] = zdot(zbuf[3], upper).reshape(cube)
-    wait1()
-    total1 = jnp.sum(sum1[...], axis=0)
-    part[1] = total1
-    sum2[q] = total1
-    start2()
-
-    planes(X0 + 1, X0 + PX - 1, lambda x, _: diagonal(x, Y0, PY), 2)
-
-    ph_recv()
-
-    def sides(body, lo, hi):
-        def both_sides(x, _):
-            return body(x, lo, 8) + body(x, hi, 8)
-
-        return both_sides
-
-    planes(X0, X0 + PX, sides(conductivity, 0, FY - 8), 4)
-    for lo in (X0 - W, X0 + PX):
-        planes(lo, lo + W, lambda x, _: conductivity(x, 0, FY), 3)
-    for lo, hi in ((X0 - W, X0 + 1), (X0 + PX - 1, X0 + PX + W - 1)):
-        planes(lo, hi, lambda x, _: faces(x, R0, RN), 2)
-    planes(X0 + 1, X0 + PX - 1, sides(faces, R0, R0 + RN - 8), 7)
-
-    zbuf[4, pl.ds(0, CY)] = jnp.concatenate([pair(wx, h, X0 - 1) for h in range(2)], axis=1)
-    zbuf[4, pl.ds(CY, CY)] = jnp.concatenate([pair(wx, h, X0 + PX - 1) for h in range(2)], axis=1)
-    for i in range(CX):
-        for k, row in enumerate((Y0 - 1, Y0 + PY - 1)):
-            for h in range(2):
-                zbuf[4, pl.ds(2 * CY + k * CX + i, 1), pl.ds(h * LANES, LANES)] = (
-                    wy[h, X0 + 2 * i, pl.ds(row, 1)] + wy[h, X0 + 2 * i + 1, pl.ds(row, 1)]
-                )
-    rim = zdot(zbuf[4, pl.ds(0, 2 * CY + 2 * CX)], both)
-    eb[0, pl.ds(CY0, CY)] = rim[:CY]
-    eb[1, pl.ds(CY0, CY)] = rim[CY : 2 * CY]
-    for i in range(CX):
-        for k in range(2):
-            j = 2 * CY + k * CX + i
-            nb[CX0 + i, pl.ds(k, 1)] = rim[j : j + 1]
-    rim_start()
+    planes(0, CX + 1, coarse_parts, 3)
+
+    flat = pl.ds(0, CX * CS)
+    center = zdot(zbuf[0], both) + zdot(zbuf[3], outer)
+    safe = jnp.where(center > 0.0, center, 1.0)
+    d = lax.rsqrt(safe)
+    d = jnp.where(center > 0.0, d * (1.5 - 0.5 * safe * d * d), 0.0)
+    cc[...] = d.reshape(CX + 1, CS, LANES)
+    weights = [zdot(zbuf[k, flat], m) for k, m in ((1, both), (2, both), (3, upper))]
+    for k in range(3):
+        zbuf[k, flat, pl.ds(0, LANES)] = weights[k]
+
+    def scale(i, _):
+        x = CX0 + i
+        at, to = pl.ds(0, CY), pl.ds(CY0, CY)
+        src_rows = pl.ds(pl.multiple_of(i * CS, 8), CY)
+        mine = cc[i, at]
+        beside = (cc[i + 1, at], cc[i, pl.ds(1, CY)], pltpu.roll(mine, LANES - 1, 1))
+        stores = [(near, (x, to), mine)]
+        for k in range(3):
+            value = zbuf[k, src_rows, pl.ds(0, LANES)] * mine * beside[k]
+            stores.append((cw, (k, x, to), value))
+        return stores
+
+    planes(0, CX, scale, 4)
+
+    cw_start()
 
     for lo, hi in ((X0 - W + 1, X0 + 1), (X0 + PX - 1, X0 + PX + W - 1)):
         planes(lo, hi, lambda x, _: diagonal(x, R0, RN), 3)
@@ -396,7 +392,6 @@
     total = jnp.sum(sum2[...], axis=0)
     average = jnp.sum(total, axis=1, keepdims=True) * (1.0 / (PX * ns * PY * ng * 2 * LANES))
     src_recv()
-    cw_start()
 
     rows = pl.ds(R0, RN)
 
@@ -408,7 +403,7 @@
             stores.append((pa, (h, x, rows), di[h, x, rows] * f))
         return stores
 
-    planes(X0 - W + 1, X0 + PX + W - 1, first_sweep, 2)
+    planes(X0 - W + 1, X0 + PX + W - 1, first_sweep, 4)
 
     def beside_sum(p, x, r0, n):
         mid, above, below = pl.ds(r0, n), pl.ds(r0 + 1, n), pl.ds(r0 - 1, n)
@@ -441,7 +436,7 @@
         v, t = beside_sum(p, x, Y0, PY)
         return v, [fo[h, x, mid] - dg[h, x, mid] * v[h] + t[h] for h in range(2)]
 
-    planes(X0 - 1, X0 + PX + 1, sweep(pa, pb), 2)
+    planes(X0 - 1, X0 + PX + 1, sweep(pa, pb), 6)
 
     def restrict(i, slot):
         a = X0 + 2 * i
@@ -457,63 +452,40 @@
             stores.append((zbuf, (4, dst, pl.ds(h * LANES, LANES)), halves_y))
         return stores
 
-    planes(0, CX, restrict, 2)
-    rem[own] = zdot(zbuf[4], both).reshape(cube)
+    planes(0, CX, restrict, 4)
+    coarse_forcing = zdot(zbuf[4, pl.ds(0, CX * CY)], both).reshape(CX, CY, LANES)
+    rem[pl.ds(CX0, CX), pl.ds(CY0, CY)] = coarse_forcing * cc[pl.ds(0, CX), pl.ds(0, CY)]
     rem_start()
     p_start()
+    near_start()
     for x in (X0 - 1, X0 + PX):
         pc[:, x, mid] = pb[:, x, mid]
 
     theta = (UPPER + LOWER) / 2.0
     delta = (UPPER - LOWER) / 2.0
     ratio = delta / theta
+    body_rows = pl.ds(1, GY - 2)
     cw_recv()
-    cw_sent()
-    rim_recv()
-    body_rows = pl.ds(1, GY - 2)
-    for k, x in enumerate((CX0 - 1, CX0 + CX - 1)):
-        east = eb[k, body_rows]
-        cw[1, x, body_rows] = east
-        for j in (x, x + 1):
-            cw[0, j, body_rows] = cw[0, j, body_rows] + east
-
-    def rim_rows(x, _):
-        stores = []
-        for k, r in enumerate((CY0 - 1, CY0 + CY - 1)):
-            north = nb[x, pl.ds(k, 1)]
-            stores.append((cw, (2, x, pl.ds(r, 1)), north))
-            for j in (r, r + 1):
-                stores.append((cw, (0, x, pl.ds(j, 1)), cw[0, x, pl.ds(j, 1)] + north))
-        return stores
-
-    planes(0, GX, rim_rows, 2)
-
-    def invert(x, _):
-        c = cw[0, x, body_rows]
-        c = jnp.where(c > 0.0, 1.0 / jnp.where(c > 0.0, c, 1.0), 0.0)
-        return [(cinv, (x, body_rows), c)]
-
-    planes(0, GX, invert, 2)
     rem_recv()
     rem_sent()
 
     def first_heading(x, _):
-        heading = rem[x, body_rows] * cinv[x, body_rows] * (1.0 / theta)
+        heading = rem[x, body_rows] * (1.0 / theta)
         return [(ha, (x, body_rows), heading), (cor, (x, body_rows), heading)]
 
-    planes(0, GX, first_heading, 2)
+    planes(0, GX, first_heading, 6)
 
     def coarse_step(old, new, r0, n, keep, add):
         mid, above, below = pl.ds(r0, n), pl.ds(r0 + 1, n), pl.ds(r0 - 1, n)
 
         def body(x, _):
             v = old[x, mid]
-            u = cw[3, x, mid]
-            t = cw[1, x, mid] * old[x + 1, mid] + cw[1, x - 1, mid] * old[x - 1, mid]
-            t = t + cw[2, x, mid] * old[x, above] + cw[2, x, below] * old[x, below]
+            u = cw[2, x, mid]
+            t = cw[0, x, mid] * old[x + 1, mid] + cw[0, x - 1, mid] * old[x - 1, mid]
+            t = t + cw[1, x, mid] * old[x, above] + cw[1, x, below] * old[x, below]
             t = t + u * pltpu.roll(v, LANES - 1, 1) + pltpu.roll(u * v, 1, 1)
-            left = rem[x, mid] - (cw[0, x, mid] * v - t)
-            heading = keep * v + add * (left * cinv[x, mid])
+            left = rem[x, mid] - (v - t)
+            heading = keep * v + add * left
             return [
                 (rem, (x, mid), left),
                 (new, (x, mid), heading),
@@ -536,7 +508,9 @@
 
     spread = lane_map(LANES, 2 * LANES, lambda i, o: o // 2 == i)
     top = CX + 4
-    picked = cor[pl.ds(CX0 - 2, top), pl.ds(CY0 - 2, CY + 8)]
+    near_recv()
+    region = (pl.ds(CX0 - 2, top), pl.ds(CY0 - 2, CY + 8))
+    picked = cor[region] * near[region]
     wide[...] = zdot(picked.reshape(top * (CY + 8), LANES), spread)
     p_recv()
 
@@ -551,10 +525,10 @@
                 stores.append((pc, (h, x + k, rows), pc[h, x + k, rows] + ebuf[slot, h, rows]))
         return stores
 
-    planes(0, top, prolong, 2)
-    planes(X0 - W + 1, X0 + PX + W - 1, sweep(pc, pa), 2)
+    planes(0, top, prolong, 4)
+    planes(X0 - W + 1, X0 + PX + W - 1, sweep(pc, pa), 5)
     p_sent()
-    planes(X0 - 1, X0 + PX + 1, sweep(pa, pb), 2)
+    planes(X0 - 1, X0 + PX + 1, sweep(pa, pb), 6)
 
     def finish(x, _):
         v, r = residual(pb, x)
@@ -564,10 +538,11 @@
             stores += [(out_p, at, v[h]), (out_r, at, r[h])]
         return stores
 
-    planes(X0, X0 + PX, finish, 2)
+    planes(X0, X0 + PX, finish, 4)
     ph_sent()
     src_sent()
-    rim_sent()
+    cw_sent()
+    near_sent()
 
 
 def write_out(p, r, out_p, out_r, sem):
@@ -582,18 +557,15 @@
     ns, ng = lax.axis_size("space"), lax.axis_size("group")
     fine = (2, FX, FY, LANES)
     coarse = (GX, GY, LANES)
-    flat = CX * CY
     vmem = pltpu.VMEM
     scratch = [vmem(fine, jnp.int32)]
     scratch += [vmem(fine, F32)] * 11
-    scratch += [vmem((4,) + coarse, F32)]
+    scratch += [vmem((3,) + coarse, F32), vmem((CX + 1, CS, LANES), F32)]
     scratch += [vmem(coarse, F32)] * 5
     scratch += [
-        vmem((2, GY, LANES), F32),
-        vmem((GX, 2, LANES), F32),
-        vmem((5, flat, 2 * LANES), F32),
-        vmem((2, 2, PY, LANES), F32),
-        vmem((2, 2, FY, LANES), F32),
+        vmem((5, (CX + 1) * CS, 2 * LANES), F32),
+        vmem((4, 2, PY, LANES), F32),
+        vmem((4, 2, FY, LANES), F32),
         vmem(((CX + 4) * (CY + 8), 2 * LANES), F32),
         vmem((2, 1, LANES), F32),
         vmem((4 * ng, 1, LANES), F32),

time: 52.3 us -> 48.9 us (0.935)
  Pallas kernels: 48.5 us -> 45.2 us
    pallas_call x1, Pallas kernels: 47.2 us -> 43.9 us  [per_device(): pl.pallas_call(functools.partial(kernel, ns, ng), out_shape=out_shape, in...]
where the time goes in v3:
time: 48.9 us; the launch traced here: 48.3 us
  Pallas kernels  45.2 us (92%)
  local copies, waits for them, and re-layouts  2.44 us (5%)
  between operations  0.65 us (1%)
    pallas_call x1, Pallas kernels, per_device(): pl.pallas_call(functools.partial(kernel, ns, ng), out_shape=out_shape, in...  43.9 us
    unnamed x4, local copies, waits for them, and re-layouts  2.44 us
    pallas_call x1, Pallas kernels, per_device(): pl.pallas_call(write_out, out_shape=out_shape, in_specs=[pl.BlockSpec(mem...  1.33 us

profile of v3, /device:TPU:9, one launch (start us, length us, event | category | flops | bytes accessed | tf_op | source)
XLA Modules:
  0.0 48.3 jit_solution(7841590093595785875)
XLA Ops:
  0.6 0.0 copy-start
  0.6 1.2 %copy-done = f32[16,64,256]{2,1,0:T(8,128)S(1)} copy-done((f32[16,64,256]{2,1,0:T(8,128)S(1)}, f32[16,64,256]{2,1,0:T(8,128)}, u32[]{:S(2)}) %copy-start) | copy-done | bytes 1048600
  1.9 0.0 copy-start.1
  1.9 1.2 %copy-done.1 = s32[16,64,256]{2,1,0:T(8,128)S(1)} copy-done((s32[16,64,256]{2,1,0:T(8,128)S(1)}, s32[16,64,256]{2,1,0:T(8,128)}, u32[]{:S(2)}) %copy-start.1) | copy-done | bytes 1048600
  3.1 43.9 %shard_map.41 = (f32[16,64,256]{2,1,0:T(8,128)S(1)}, f32[16,64,256]{2,1,0:T(8,128)S(1)}) custom-call(f32[16,64,256]{2,1,0:T(8,128)S(1)} %copy-done, s32[16,64,256]{2,1,0:T(8,128)S(1)} %copy-done.1), custom_call_target="tpu_custom_call" | custom-call | tf_op jit(solution)/shard_map/pallas_call | solution.py:580
  47.0 1.3 %shard_map.42 = (f32[16,64,256]{2,1,0:T(8,128)}, f32[16,64,256]{2,1,0:T(8,128)}) custom-call(f32[16,64,256]{2,1,0:T(8,128)S(1)} %get-tuple-element.4.p, f32[16,64,256]{2,1,0:T(8,128)S(1)} %get-tuple-element.5.r), custom_call_target="tpu_custom_call" | custom-call | tf_op jit(solution)/shard_map/pallas_call | solution.py:590
Async XLA Ops:
  0.6 1.2 %copy-start = (f32[16,64,256]{2,1,0:T(8,128)S(1)}, f32[16,64,256]{2,1,0:T(8,128)}, u32[]{:S(2)}) copy-start(f32[16,64,256]{2,1,0:T(8,128)} %source_hbm.1) | copy-start | bytes 3145732
  1.9 1.2 %copy-start.1 = (s32[16,64,256]{2,1,0:T(8,128)S(1)}, s32[16,64,256]{2,1,0:T(8,128)}, u32[]{:S(2)}) copy-start(s32[16,64,256]{2,1,0:T(8,128)} %phases_hbm.1) | copy-start | bytes 3145732

commit v4 on v3

--- a/solution.py
+++ b/solution.py
@@ -24,13 +24,13 @@
 W = 3
 R0, RN = 4, 72
 CX, CY = PX // 2, PY // 2
-CW, CX0, CY0 = 7, 7, 8
+CW, CX0, CY0 = 5, 5, 8
 GX, GY = CX + 2 * CX0, CY + 2 * CY0
 CS = CY + 8
 DIRS = [(-1, 0), (1, 0), (0, -1), (0, 1), (-1, -1), (-1, 1), (1, -1), (1, 1)]
 MESSAGES = 8 * 4 + 16 + 12
 NO_CELL = 1 << 20
-NEAR, NEAR_ROWS, FAR_ROWS = 3, 6, 3
+NEAR, NEAR_ROWS, FAR_ROWS = 2, 4, 2
 
 
 def spans(step, start, size, near, far):
@@ -80,7 +80,7 @@
 def kernel(
     ns, ng, source_hbm, phases_hbm, out_p, out_r,
     ph, src, kap, wx, wy, wz, dg, di, fo, pa, pb, pc,
-    cw, cc, rem, ha, hb, cor, near, zbuf, ybuf, ebuf, wide,
+    cw, cc, rem, ha, hb, cor, near, zbuf, ybuf, ebuf,
     part, sum1, sum2,
     in_sem, psend, precv, send, recv,
 ):
@@ -199,8 +199,8 @@
                 boxes = [(0, NEAR, NEAR_ROWS, None), (NEAR, CW - 1, FAR_ROWS, None)]
             else:
                 boxes = [(0, far, CW, span) for span, far in parts or [(None, CW)]]
-            for near, far, count, span in boxes:
-                sx, tx = spans(dx, CX0, CX, near, far)
+            for after, far, count, span in boxes:
+                sx, tx = spans(dx, CX0, CX, after, far)
                 sy, ty = spans(dy, CY0, CY, 0, count)
                 lead = () if parts is None else (span or slice(None),)
                 messages.append(((dx, dy), a.at[lead + (sx, sy)], a.at[lead + (tx, ty)]))
@@ -374,7 +374,7 @@
         src_rows = pl.ds(pl.multiple_of(i * CS, 8), CY)
         mine = cc[i, at]
         beside = (cc[i + 1, at], cc[i, pl.ds(1, CY)], pltpu.roll(mine, LANES - 1, 1))
-        stores = [(near, (x, to), mine)]
+        stores = []
         for k in range(3):
             value = zbuf[k, src_rows, pl.ds(0, LANES)] * mine * beside[k]
             stores.append((cw, (k, x, to), value))
@@ -420,13 +420,16 @@
             sums.append(t + z[h] * up[h] + down[h])
         return v, sums
 
-    def sweep(old, new):
+    def sweep(old, new, *strips):
         def body(x, _):
-            v, t = beside_sum(old, x, R0, RN)
-            return [
-                (new, (h, x, rows), (1.0 - RELAX) * v[h] + di[h, x, rows] * (fo[h, x, rows] + t[h]))
-                for h in range(2)
-            ]
+            stores = []
+            for r0, n in strips or ((R0, RN),):
+                at = pl.ds(r0, n)
+                v, t = beside_sum(old, x, r0, n)
+                for h in range(2):
+                    value = (1.0 - RELAX) * v[h] + di[h, x, at] * (fo[h, x, at] + t[h])
+                    stores.append((new, (h, x, at), value))
+            return stores
 
         return body
 
@@ -456,16 +459,15 @@
     coarse_forcing = zdot(zbuf[4, pl.ds(0, CX * CY)], both).reshape(CX, CY, LANES)
     rem[pl.ds(CX0, CX), pl.ds(CY0, CY)] = coarse_forcing * cc[pl.ds(0, CX), pl.ds(0, CY)]
     rem_start()
-    p_start()
-    near_start()
     for x in (X0 - 1, X0 + PX):
         pc[:, x, mid] = pb[:, x, mid]
 
     theta = (UPPER + LOWER) / 2.0
     delta = (UPPER - LOWER) / 2.0
     ratio = delta / theta
-    body_rows = pl.ds(1, GY - 2)
+    body_rows = pl.ds(CY0 - CW, CY + 2 * CW)
     cw_recv()
+    p_start()
     rem_recv()
     rem_sent()
 
@@ -502,31 +504,60 @@
         step = coarse_step(
             old, new, CY0 - halo, CY + 2 * halo, following * ratio, 2.0 * following / delta
         )
-        planes(lo, hi, step, {20: 5, 18: 6, 16: 4, 14: 7, 12: 6}[hi - lo])
+        planes(lo, hi, step, {16: 4, 14: 7, 12: 6, 10: 5, 8: 4}[hi - lo])
         ratio = following
         old, new = new, old
 
+    inside = (pl.ds(CX0, CX), pl.ds(CY0, CY))
+    near[inside] = cor[inside] * cc[pl.ds(0, CX), pl.ds(0, CY)]
+    near_start()
     spread = lane_map(LANES, 2 * LANES, lambda i, o: o // 2 == i)
-    top = CX + 4
+
+    def prolong(part, c, r, n, slot):
+        x, r0 = X0 + 2 * (c - CX0), Y0 + 2 * (r - CY0)
+        at = pl.ds(r0, 2 * n)
+        stores = []
+        for h in range(2):
+            value = part[:, h * LANES : (h + 1) * LANES]
+            ebuf[slot, h, pl.ds(r0, n, stride=2)] = value
+            ebuf[slot, h, pl.ds(r0 + 1, n, stride=2)] = value
+            for k in range(2):
+                stores.append((pc, (h, x + k, at), pc[h, x + k, at] + ebuf[slot, h, at]))
+        return stores
+
+    zbuf[0, pl.ds(0, CX * CY)] = zdot(near[inside].reshape(CX * CY, LANES), spread)
+
+    def prolong_inside(i, slot):
+        part = zbuf[0, pl.ds(pl.multiple_of(i * CY, CY), CY)]
+        return prolong(part, CX0 + i, CY0, CY, slot)
+
+    planes(0, CX, prolong_inside, 4)
+    edge = 12
+    planes(X0 + 1, X0 + PX - 1, sweep(pc, pa, (R0 + edge, RN - 2 * edge)), 7)
+
+    p_recv()
     near_recv()
-    region = (pl.ds(CX0 - 2, top), pl.ds(CY0 - 2, CY + 8))
-    picked = cor[region] * near[region]
-    wide[...] = zdot(picked.reshape(top * (CY + 8), LANES), spread)
-    p_recv()
-
-    def prolong(c, slot):
-        x = 2 * c + X0 - 4
-        stores = []
-        for h in range(2):
-            part_h = wide[pl.ds(pl.multiple_of(c * (CY + 8), 8), CY + 4), pl.ds(h * LANES, LANES)]
-            ebuf[slot, h, pl.ds(R0, RN // 2, stride=2)] = part_h
-            ebuf[slot, h, pl.ds(R0 + 1, RN // 2, stride=2)] = part_h
-            for k in range(2):
-                stores.append((pc, (h, x + k, rows), pc[h, x + k, rows] + ebuf[slot, h, rows]))
-        return stores
-
-    planes(0, top, prolong, 4)
-    planes(X0 - W + 1, X0 + PX + W - 1, sweep(pc, pa), 5)
+    tall = CY + 8
+    sides_x = (CX0 - 2, CX0 - 1, CX0 + CX, CX0 + CX + 1)
+    for k, c in enumerate(sides_x):
+        zbuf[1, pl.ds(k * tall, tall)] = zdot(near[c, pl.ds(CY0 - 2, tall)], spread)
+    for k, r in enumerate((CY0 - 8, CY0 + CY)):
+        strip = near[pl.ds(CX0, CX), pl.ds(r, 8)].reshape(CX * 8, LANES)
+        zbuf[2, pl.ds(k * CX * 8, CX * 8)] = zdot(strip, spread)
+    for k, c in enumerate(sides_x):
+        part = zbuf[1, pl.ds(k * tall, CY + 4)]
+        for ref, at, value in prolong(part, c, CY0 - 2, CY + 4, k):
+            ref[at] = value
+
+    for i in range(CX):
+        low = zbuf[2, pl.ds(i * 8 + 6, 2)]
+        high = zbuf[2, pl.ds(CX * 8 + i * 8, 2)]
+        stores = prolong(low, CX0 + i, CY0 - 2, 2, i % 4)
+        for ref, at, value in stores + prolong(high, CX0 + i, CY0 + CY, 2, i % 4):
+            ref[at] = value
+    for lo, hi in ((X0 - W + 1, X0 + 1), (X0 + PX - 1, X0 + PX + W - 1)):
+        planes(lo, hi, sweep(pc, pa), 3)
+    planes(X0 + 1, X0 + PX - 1, sweep(pc, pa, (R0, edge), (R0 + RN - edge, edge)), 7)
     p_sent()
     planes(X0 - 1, X0 + PX + 1, sweep(pa, pb), 6)
 
@@ -566,7 +597,6 @@
         vmem((5, (CX + 1) * CS, 2 * LANES), F32),
         vmem((4, 2, PY, LANES), F32),
         vmem((4, 2, FY, LANES), F32),
-        vmem(((CX + 4) * (CY + 8), 2 * LANES), F32),
         vmem((2, 1, LANES), F32),
         vmem((4 * ng, 1, LANES), F32),
         vmem((ns // 4, 1, LANES), F32),

time: 48.9 us -> 44.3 us (0.906)
  Pallas kernels: 45.2 us -> 41 us
    pallas_call x1, Pallas kernels: 43.9 us -> 39.7 us  [per_device(): pl.pallas_call(functools.partial(kernel, ns, ng), out_shape=out_shape, in...]
where the time goes in v4:
time: 44.3 us; the launch traced here: 44.1 us
  Pallas kernels  41 us (93%)
  local copies, waits for them, and re-layouts  2.44 us (6%)
  between operations  0.65 us (1%)
    pallas_call x1, Pallas kernels, per_device(): pl.pallas_call(functools.partial(kernel, ns, ng), out_shape=out_shape, in...  39.7 us
    unnamed x4, local copies, waits for them, and re-layouts  2.44 us
    pallas_call x1, Pallas kernels, per_device(): pl.pallas_call(write_out, out_shape=out_shape, in_specs=[pl.BlockSpec(mem...  1.33 us

profile of v4, /device:TPU:9, one launch (start us, length us, event | category | flops | bytes accessed | tf_op | source)
XLA Modules:
  0.0 44.1 jit_solution(3326811574185098582)
XLA Ops:
  0.6 0.0 copy-start
  0.6 1.2 %copy-done = f32[16,64,256]{2,1,0:T(8,128)S(1)} copy-done((f32[16,64,256]{2,1,0:T(8,128)S(1)}, f32[16,64,256]{2,1,0:T(8,128)}, u32[]{:S(2)}) %copy-start) | copy-done | bytes 1048600
  1.9 0.0 copy-start.1
  1.9 1.2 %copy-done.1 = s32[16,64,256]{2,1,0:T(8,128)S(1)} copy-done((s32[16,64,256]{2,1,0:T(8,128)S(1)}, s32[16,64,256]{2,1,0:T(8,128)}, u32[]{:S(2)}) %copy-start.1) | copy-done | bytes 1048600
  3.1 39.7 %shard_map.41 = (f32[16,64,256]{2,1,0:T(8,128)S(1)}, f32[16,64,256]{2,1,0:T(8,128)S(1)}) custom-call(f32[16,64,256]{2,1,0:T(8,128)S(1)} %copy-done, s32[16,64,256]{2,1,0:T(8,128)S(1)} %copy-done.1), custom_call_target="tpu_custom_call" | custom-call | tf_op jit(solution)/shard_map/pallas_call | solution.py:610
  42.8 1.3 %shard_map.42 = (f32[16,64,256]{2,1,0:T(8,128)}, f32[16,64,256]{2,1,0:T(8,128)}) custom-call(f32[16,64,256]{2,1,0:T(8,128)S(1)} %get-tuple-element.4.p, f32[16,64,256]{2,1,0:T(8,128)S(1)} %get-tuple-element.5.r), custom_call_target="tpu_custom_call" | custom-call | tf_op jit(solution)/shard_map/pallas_call | solution.py:620
Async XLA Ops:
  0.6 1.2 %copy-start = (f32[16,64,256]{2,1,0:T(8,128)S(1)}, f32[16,64,256]{2,1,0:T(8,128)}, u32[]{:S(2)}) copy-start(f32[16,64,256]{2,1,0:T(8,128)} %source_hbm.1) | copy-start | bytes 3145732
  1.9 1.2 %copy-start.1 = (s32[16,64,256]{2,1,0:T(8,128)S(1)}, s32[16,64,256]{2,1,0:T(8,128)}, u32[]{:S(2)}) copy-start(s32[16,64,256]{2,1,0:T(8,128)} %phases_hbm.1) | copy-start | bytes 3145732

commit v5 on v4

--- a/solution.py
+++ b/solution.py
@@ -77,9 +77,34 @@
         run(lo + whole * k, (hi - lo) % k)
 
 
+def beside_sum(p, weights, x, r0, n):
+    wx, wy, wz = weights
+    lane = lax.broadcasted_iota(jnp.int32, (1, LANES), 1)
+    first, last = lane == 0, lane == LANES - 1
+    mid, above, below = pl.ds(r0, n), pl.ds(r0 + 1, n), pl.ds(r0 - 1, n)
+    v = [p[h, x, mid] for h in range(2)]
+    z = [wz[h, x, mid] for h in range(2)]
+    up = [pltpu.roll(v[h], LANES - 1, 1) for h in range(2)]
+    down = [pltpu.roll(z[h] * v[h], 1, 1) for h in range(2)]
+    up[0] = jnp.where(last, up[1], up[0])
+    down = [jnp.where(first, 0.0, down[0]), jnp.where(first, down[0], down[1])]
+    sums = []
+    for h in range(2):
+        t = wx[h, x, mid] * p[h, x + 1, mid] + wx[h, x - 1, mid] * p[h, x - 1, mid]
+        t = t + wy[h, x, mid] * p[h, x, above] + wy[h, x, below] * p[h, x, below]
+        sums.append(t + z[h] * up[h] + down[h])
+    return v, sums
+
+
+def residual(p, weights, fo, dg, x):
+    mid = pl.ds(Y0, PY)
+    v, t = beside_sum(p, weights, x, Y0, PY)
+    return v, [fo[h, x, mid] - dg[h, x, mid] * v[h] + t[h] for h in range(2)]
+
+
 def kernel(
-    ns, ng, source_hbm, phases_hbm, out_p, out_r,
-    ph, src, kap, wx, wy, wz, dg, di, fo, pa, pb, pc,
+    ns, ng, source_hbm, phases_hbm, wx, wy, wz, dg, fo, pb,
+    ph, src, kap, di, pa, pc,
     cw, cc, rem, ha, hb, cor, near, zbuf, ybuf, ebuf,
     part, sum1, sum2,
     in_sem, psend, precv, send, recv,
@@ -304,7 +329,6 @@
     start2, wait2 = gather_part(1, sum2, nq, q, peer2)
     start1()
     ph_start()
-    src_start()
 
     planes(X0, X0 + PX, lambda x, _: faces(x, Y0, PY), 4)
 
@@ -313,6 +337,7 @@
     part[1] = total1
     sum2[q] = total1
     start2()
+    src_start()
 
     planes(X0 + 1, X0 + PX - 1, lambda x, _: diagonal(x, Y0, PY), 7)
 
@@ -405,27 +430,12 @@
 
     planes(X0 - W + 1, X0 + PX + W - 1, first_sweep, 4)
 
-    def beside_sum(p, x, r0, n):
-        mid, above, below = pl.ds(r0, n), pl.ds(r0 + 1, n), pl.ds(r0 - 1, n)
-        v = [p[h, x, mid] for h in range(2)]
-        z = [wz[h, x, mid] for h in range(2)]
-        up = [pltpu.roll(v[h], LANES - 1, 1) for h in range(2)]
-        down = [pltpu.roll(z[h] * v[h], 1, 1) for h in range(2)]
-        up[0] = jnp.where(last, up[1], up[0])
-        down = [jnp.where(first, 0.0, down[0]), jnp.where(first, down[0], down[1])]
-        sums = []
-        for h in range(2):
-            t = wx[h, x, mid] * p[h, x + 1, mid] + wx[h, x - 1, mid] * p[h, x - 1, mid]
-            t = t + wy[h, x, mid] * p[h, x, above] + wy[h, x, below] * p[h, x, below]
-            sums.append(t + z[h] * up[h] + down[h])
-        return v, sums
-
     def sweep(old, new, *strips):
         def body(x, _):
             stores = []
             for r0, n in strips or ((R0, RN),):
                 at = pl.ds(r0, n)
-                v, t = beside_sum(old, x, r0, n)
+                v, t = beside_sum(old, (wx, wy, wz), x, r0, n)
                 for h in range(2):
                     value = (1.0 - RELAX) * v[h] + di[h, x, at] * (fo[h, x, at] + t[h])
                     stores.append((new, (h, x, at), value))
@@ -435,16 +445,12 @@
 
     mid = pl.ds(Y0, PY)
 
-    def residual(p, x):
-        v, t = beside_sum(p, x, Y0, PY)
-        return v, [fo[h, x, mid] - dg[h, x, mid] * v[h] + t[h] for h in range(2)]
-
     planes(X0 - 1, X0 + PX + 1, sweep(pa, pb), 6)
 
     def restrict(i, slot):
         a = X0 + 2 * i
-        va, ra = residual(pb, a)
-        vb, rb = residual(pb, a + 1)
+        va, ra = residual(pb, (wx, wy, wz), fo, dg, a)
+        vb, rb = residual(pb, (wx, wy, wz), fo, dg, a + 1)
         dst = pl.ds(pl.multiple_of(i * CY, CY), CY)
         stores = []
         for h in range(2):
@@ -561,25 +567,30 @@
     p_sent()
     planes(X0 - 1, X0 + PX + 1, sweep(pa, pb), 6)
 
-    def finish(x, _):
-        v, r = residual(pb, x)
-        stores = []
-        for h in range(2):
-            at = (x - X0, pl.ds(0, PY), pl.ds(h * LANES, LANES))
-            stores += [(out_p, at, v[h]), (out_r, at, r[h])]
-        return stores
-
-    planes(X0, X0 + PX, finish, 4)
     ph_sent()
     src_sent()
     cw_sent()
     near_sent()
 
 
-def write_out(p, r, out_p, out_r, sem):
-    copies = [pltpu.make_async_copy(p, out_p, sem.at[0]), pltpu.make_async_copy(r, out_r, sem.at[1])]
-    for copy in copies:
-        copy.start()
+def finish(wx, wy, wz, dg, fo, pb, out_p, out_r, res, sem):
+    copies = []
+    for h in range(2):
+        cols = pl.ds(h * LANES, LANES)
+        block = pb.at[h, pl.ds(X0, PX), pl.ds(Y0, PY)]
+        copies.append(pltpu.make_async_copy(block, out_p.at[:, :, cols], sem.at[h]))
+        copies[-1].start()
+    quarter = PX // 4
+    for k in range(4):
+        stores = []
+        for x in range(k * quarter, (k + 1) * quarter):
+            _, r = residual(pb, (wx, wy, wz), fo, dg, X0 + x)
+            stores += [((x, pl.ds(0, PY), pl.ds(h * LANES, LANES)), r[h]) for h in range(2)]
+        for at, value in stores:
+            res[at] = value
+        part = pl.ds(k * quarter, quarter)
+        copies.append(pltpu.make_async_copy(res.at[part], out_r.at[part], sem.at[2 + k]))
+        copies[-1].start()
     for copy in copies:
         copy.wait()
 
@@ -590,7 +601,7 @@
     coarse = (GX, GY, LANES)
     vmem = pltpu.VMEM
     scratch = [vmem(fine, jnp.int32)]
-    scratch += [vmem(fine, F32)] * 11
+    scratch += [vmem(fine, F32)] * 5
     scratch += [vmem((3,) + coarse, F32), vmem((CX + 1, CS, LANES), F32)]
     scratch += [vmem(coarse, F32)] * 5
     scratch += [
@@ -606,25 +617,24 @@
         pltpu.SemaphoreType.DMA((MESSAGES,)),
         pltpu.SemaphoreType.DMA((MESSAGES,)),
     ]
-    out_shape = [jax.ShapeDtypeStruct(source.shape, F32)] * 2
-    pressure, residual = pl.pallas_call(
+    fields = pl.pallas_call(
         functools.partial(kernel, ns, ng),
-        out_shape=out_shape,
+        out_shape=[jax.ShapeDtypeStruct(fine, F32)] * 6,
         in_specs=[pl.BlockSpec(memory_space=pltpu.HBM)] * 2,
-        out_specs=[pl.BlockSpec(memory_space=pltpu.VMEM)] * 2,
+        out_specs=[pl.BlockSpec(memory_space=pltpu.VMEM)] * 6,
         scratch_shapes=scratch,
         compiler_params=pltpu.CompilerParams(
             collective_id=0, has_side_effects=True, vmem_limit_bytes=40 * 2**20
         ),
     )(source, phases)
     return pl.pallas_call(
-        write_out,
-        out_shape=out_shape,
-        in_specs=[pl.BlockSpec(memory_space=pl.ANY)] * 2,
+        finish,
+        out_shape=[jax.ShapeDtypeStruct(source.shape, F32)] * 2,
+        in_specs=[pl.BlockSpec(memory_space=pltpu.VMEM)] * 6,
         out_specs=[pl.BlockSpec(memory_space=pl.ANY)] * 2,
-        scratch_shapes=[pltpu.SemaphoreType.DMA((2,))],
-        compiler_params=pltpu.CompilerParams(vmem_limit_bytes=2**20),
-    )(pressure, residual)
+        scratch_shapes=[vmem(source.shape, F32), pltpu.SemaphoreType.DMA((6,))],
+        compiler_params=pltpu.CompilerParams(vmem_limit_bytes=16 * 2**20),
+    )(*fields)
 
 
 def solution(mesh):

time: 44.3 us -> 43.2 us (0.975)
  Pallas kernels: 41 us -> 39.9 us
    pallas_call x2, Pallas kernels: 41 us -> 39.9 us  [the longest x1 38.3 us: per_device(): pl.pallas_call(functools.partial(kernel, ns, ng), out_shape=[jax.ShapeDty...]
where the time goes in v5:
time: 43.2 us; the launch traced here: 43 us
  Pallas kernels  39.9 us (92%)
  local copies, waits for them, and re-layouts  2.44 us (6%)
  between operations  0.65 us (2%)
    pallas_call x1, Pallas kernels, per_device(): pl.pallas_call(functools.partial(kernel, ns, ng), out_shape=[jax.ShapeDty...  38.3 us
    unnamed x4, local copies, waits for them, and re-layouts  2.44 us
    pallas_call x1, Pallas kernels, per_device(): pl.pallas_call(finish, out_shape=[jax.ShapeDtypeStruct(source.shape, F32)...  1.6 us

profile of v5, /device:TPU:9, one launch (start us, length us, event | category | flops | bytes accessed | tf_op | source)
XLA Modules:
  0.0 43.0 jit_solution(1633559085126428495)
XLA Ops:
  0.6 0.0 copy-start
  0.6 1.2 %copy-done = f32[16,64,256]{2,1,0:T(8,128)S(1)} copy-done((f32[16,64,256]{2,1,0:T(8,128)S(1)}, f32[16,64,256]{2,1,0:T(8,128)}, u32[]{:S(2)}) %copy-start) | copy-done | bytes 1048600
  1.9 0.0 copy-start.1
  1.9 1.2 %copy-done.1 = s32[16,64,256]{2,1,0:T(8,128)S(1)} copy-done((s32[16,64,256]{2,1,0:T(8,128)S(1)}, s32[16,64,256]{2,1,0:T(8,128)}, u32[]{:S(2)}) %copy-start.1) | copy-done | bytes 1048600
  3.1 38.3 %shard_map.41 = (f32[2,24,80,128]{3,2,1,0:T(8,128)S(1)}, f32[2,24,80,128]{3,2,1,0:T(8,128)S(1)}, f32[2,24,80,128]{3,2,1,0:T(8,128)S(1)}, f32[2,24,80,128]{3,2,1,...) custom-call(f32[16,64,256]{2,1,0:T(8,128)S(1)} %copy-done, s32[16,64,256]{2,1,0:T(8,128)S(1)} %copy-done.1), custom_call_target="tpu_custom_call" | custom-call | tf_op jit(solution)/shard_map/pallas_call | solution.py:620
  41.4 1.6 %shard_map.42 = (f32[16,64,256]{2,1,0:T(8,128)}, f32[16,64,256]{2,1,0:T(8,128)}) custom-call(f32[2,24,80,128]{3,2,1,0:T(8,128)S(1)} %get-tuple-element.8.wx, f32[2,24,80,128]{3,2,1,0:T(8,128)S(1)} %get-tuple-element.9.wy, f32[2,24,80,128]{3,2,1,0:T(8,128)S(1)} %get-tuple-element.10.wz, f32[2,24,80,128]{3,2,1,0:T(8,128)S(1)} %get-tuple-element.11.dg, ...), custom_call_target="tpu_custom_call" | custom-call | tf_op jit(solution)/shard_map/pallas_call | solution.py:630
Async XLA Ops:
  0.6 1.2 %copy-start = (f32[16,64,256]{2,1,0:T(8,128)S(1)}, f32[16,64,256]{2,1,0:T(8,128)}, u32[]{:S(2)}) copy-start(f32[16,64,256]{2,1,0:T(8,128)} %source_hbm.1) | copy-start | bytes 3145732
  1.9 1.2 %copy-start.1 = (s32[16,64,256]{2,1,0:T(8,128)S(1)}, s32[16,64,256]{2,1,0:T(8,128)}, u32[]{:S(2)}) copy-start(s32[16,64,256]{2,1,0:T(8,128)} %phases_hbm.1) | copy-start | bytes 3145732
